TPU v7x, 256 devices: a whole 4x4x8 slice. The times are simulated.
256 devices in a mesh: ctx: 16 (over z, x_hi), tp: 8 (over y, core), dp: 2 (over x_lo).
Axes of the slice: x: 4 (x_hi: 2, x_lo: 2; x = x_hi * 2 + x_lo), y: 4, z: 8, core: 2. Of those that a mesh axis runs over, the one named last changes fastest.
Arguments:
- queries: bfloat16 [2, 4096, 3072], P('dp', 'ctx', 'tp'), may hold values from -6 to 6
- keys: bfloat16 [2, 4096, 3072], P('dp', 'ctx', 'tp'), may hold values from -6 to 6
- values: bfloat16 [2, 4096, 3072], P('dp', 'ctx', 'tp'), may hold values from -6 to 6
- out_grad: bfloat16 [2, 4096, 3072], P('dp', 'ctx', 'tp'), may hold values from -6 to 6
- depth_kernel: bfloat16 [27, 3072], P(None, 'tp'), may hold values from -1.25 to 1.25
- point_weight: bfloat16 [3072, 3072], P('tp'), may hold values from -0.109375 to 0.109375
- block_of_frame: int32 [32], replicated, may hold values from 0 to 15, never falling along the last dimension, each value on 1 to 4 neighbouring positions
Outputs:
- query_grad: bfloat16 [2, 4096, 3072], P('dp', 'ctx', 'tp')
- key_grad: bfloat16 [2, 4096, 3072], P('dp', 'ctx', 'tp')
- value_grad: bfloat16 [2, 4096, 3072], P('dp', 'ctx', 'tp')
- point_grad: float32 [3072, 3072], P('tp')
- depth_grad: float32 [27, 3072], P(None, 'tp')
Inputs may be any that keep to these rules, and one draw needn't show every extreme that they name: `block_of_frame`: block numbers never fall along the frames; a block spans 1 to 4 frames.
All inputs are finite; a program needn't handle non-finite values.
Results may differ from a plain program's by a relative error of at most 0.023.
Values may be sent and summed in bfloat16 or wider, within the bound.
A program may use at most 128 MiB of HBM per device.

v0:
```python
import math

import jax
import jax.numpy as jnp
from jax import lax
from jax.sharding import PartitionSpec as P

HD = 128
HH = 8
WW = 16


NEG = -1e30


def with_halo(cells, sides, width):
    for axis, dim in sides:
        count = lax.axis_size(axis)
        ends = count - 1
        head = lax.slice_in_dim(cells, 0, width, axis=dim)
        tail = lax.slice_in_dim(cells, cells.shape[dim] - width, cells.shape[dim], axis=dim)
        cells = jnp.concatenate(
            [
                lax.ppermute(tail, axis, [(i, (i + 1) % count) for i in range(ends)]),
                cells,
                lax.ppermute(head, axis, [((i + 1) % count, i) for i in range(ends)]),
            ],
            axis=dim,
        )
    return cells


def tap_offsets(tap_index):
    return (tap_index // 9 - 1, tap_index // 3 % 3 - 1, tap_index % 3 - 1)


def padded_grid(extended, frame_count):
    channels = extended.shape[1]
    grid = extended.astype(jnp.float32).reshape(frame_count + 2, HH, WW, channels)
    return jnp.pad(grid, ((0, 0), (1, 1), (1, 1), (0, 0)))


def depthwise(grid, kernel, frame_count, direction):
    channels = grid.shape[3]
    result = jnp.zeros((frame_count, HH, WW, channels), jnp.float32)
    for tap_index in range(27):
        frame_shift, row_shift, column_shift = tap_offsets(tap_index)
        first_frame = 1 + direction * frame_shift
        first_row = 1 + direction * row_shift
        first_column = 1 + direction * column_shift
        window = grid[
            first_frame : first_frame + frame_count,
            first_row : first_row + HH,
            first_column : first_column + WW,
        ]
        result = result + kernel[tap_index] * window
    return result.reshape(frame_count * HH * WW, channels)


def tap_sums(attn_grid, grad_grid, frame_count):
    collected = []
    for tap_index in range(27):
        frame_shift, row_shift, column_shift = tap_offsets(tap_index)
        window = attn_grid[
            1 + frame_shift : 1 + frame_shift + frame_count,
            1 + row_shift : 1 + row_shift + HH,
            1 + column_shift : 1 + column_shift + WW,
        ]
        collected.append(jnp.sum(window * grad_grid, axis=(0, 1, 2)))
    return jnp.stack(collected)


def frame_blocks(token_ids, block_of_frame, frame_size):
    frames = token_ids // frame_size
    frame_ids = jnp.arange(block_of_frame.shape[0], dtype=jnp.int32)
    return jnp.sum(
        jnp.where(frames[:, None] == frame_ids[None, :], block_of_frame[None, :], 0), axis=1
    )


def masked_scores(query_heads, key_heads, query_blocks, key_blocks, scaling):
    scores = (
        jnp.einsum("qhd,khd->hqk", query_heads, key_heads, preferred_element_type=jnp.float32)
        * scaling
    )
    return jnp.where((key_blocks[None, :] <= query_blocks[:, None])[None], scores, NEG)


def grad_tile(
    query_heads,
    grad_heads,
    log_sums,
    row_dots,
    query_blocks,
    key_heads,
    value_heads,
    key_blocks,
    scaling,
):
    scores = masked_scores(query_heads, key_heads, query_blocks, key_blocks, scaling)
    probs = jnp.exp(scores - log_sums[:, :, None])
    dprobs = jnp.einsum("qhd,khd->hqk", grad_heads, value_heads, preferred_element_type=jnp.float32)
    dscores = (probs * (dprobs - row_dots[:, :, None])).astype(jnp.bfloat16)
    part_query = (
        jnp.einsum("hqk,khd->qhd", dscores, key_heads, preferred_element_type=jnp.float32) * scaling
    )
    part_key = (
        jnp.einsum("hqk,qhd->khd", dscores, query_heads, preferred_element_type=jnp.float32)
        * scaling
    )
    part_value = jnp.einsum(
        "hqk,qhd->khd", probs.astype(jnp.bfloat16), grad_heads, preferred_element_type=jnp.float32
    )
    return (part_query, part_key, part_value)


def attend(query_heads, key_heads, value_heads, query_blocks, all_blocks, scaling):
    query_count, head_count, head_size = query_heads.shape
    key_count = key_heads.shape[0]
    block_rows = math.gcd(key_count, 512)
    start_state = (
        jnp.full((head_count, query_count), NEG, jnp.float32),
        jnp.zeros((head_count, query_count), jnp.float32),
        jnp.zeros((head_count, query_count, head_size), jnp.float32),
    )

    def attend_step(block_index, carry):
        first_row = block_index * block_rows
        key_part = lax.dynamic_slice_in_dim(key_heads, first_row, block_rows, 0)
        value_part = lax.dynamic_slice_in_dim(value_heads, first_row, block_rows, 0)
        block_ids = lax.dynamic_slice_in_dim(all_blocks, first_row, block_rows, 0)
        row_max, row_sum, weighted = carry
        scores = masked_scores(query_heads, key_part, query_blocks, block_ids, scaling)
        new_max = jnp.maximum(row_max, jnp.max(scores, axis=2))
        factor = jnp.exp(row_max - new_max)
        weights = jnp.exp(scores - new_max[:, :, None])
        row_sum = row_sum * factor + jnp.sum(weights, axis=2)
        weighted = weighted * factor[:, :, None] + jnp.einsum(
            "hqk,khd->hqd",
            weights.astype(jnp.bfloat16),
            value_part,
            preferred_element_type=jnp.float32,
        )
        return (new_max, row_sum, weighted)

    row_max, row_sum, weighted = lax.fori_loop(0, key_count // block_rows, attend_step, start_state)
    attended = (weighted / row_sum[:, :, None]).astype(jnp.bfloat16)
    return (attended, row_max + jnp.log(row_sum))


def key_sweep(
    query_heads,
    grad_heads,
    log_sums,
    row_dots,
    query_blocks,
    key_heads,
    value_heads,
    all_blocks,
    scaling,
):
    query_count, head_count, head_size = query_heads.shape
    key_count = key_heads.shape[0]
    local_width = head_count * head_size
    block_rows = math.gcd(key_count, 512)
    key_width = 2 * local_width
    start_state = (
        jnp.zeros((query_count, head_count, head_size), jnp.float32),
        jnp.zeros((key_count, key_width), jnp.float32),
    )

    def key_step(block_index, carry):
        first_row = block_index * block_rows
        key_part = lax.dynamic_slice_in_dim(key_heads, first_row, block_rows, 0)
        value_part = lax.dynamic_slice_in_dim(value_heads, first_row, block_rows, 0)
        block_ids = lax.dynamic_slice_in_dim(all_blocks, first_row, block_rows, 0)
        grad_query, key_terms = carry
        part_query, part_key, part_value = grad_tile(
            query_heads,
            grad_heads,
            log_sums,
            row_dots,
            query_blocks,
            key_part,
            value_part,
            block_ids,
            scaling,
        )
        joined = jnp.concatenate(
            [
                part_key.reshape(block_rows, local_width),
                part_value.reshape(block_rows, local_width),
            ],
            axis=1,
        )
        key_terms = lax.dynamic_update_slice_in_dim(key_terms, joined, first_row, 0)
        return (grad_query + part_query, key_terms)

    return lax.fori_loop(0, key_count // block_rows, key_step, start_state)


def local(queries, keys, values, out_grad, depth_kernel, point_weight, block_of_frame):
    frame_size = HH * WW
    scaling = 1.0 / math.sqrt(HD)
    query_rows = queries[0]
    key_rows = keys[0]
    value_rows = values[0]
    grad_rows = out_grad[0]
    token_count, local_width = query_rows.shape
    head_count = local_width // HD
    frame_count = token_count // frame_size
    kernel = depth_kernel.astype(jnp.float32)
    local_ids = lax.axis_index("ctx") * token_count + jnp.arange(token_count, dtype=jnp.int32)
    query_blocks = frame_blocks(local_ids, block_of_frame, frame_size)
    all_keys, all_values = (
        lax.all_gather(key_rows, "ctx", axis=0, tiled=True),
        lax.all_gather(value_rows, "ctx", axis=0, tiled=True),
    )
    key_count = all_keys.shape[0]
    all_blocks = frame_blocks(jnp.arange(key_count, dtype=jnp.int32), block_of_frame, frame_size)
    query_heads = query_rows.reshape(token_count, head_count, HD)
    key_heads = all_keys.reshape(key_count, head_count, HD)
    value_heads = all_values.reshape(key_count, head_count, HD)
    attended, log_sums = attend(
        query_heads, key_heads, value_heads, query_blocks, all_blocks, scaling
    )
    attended_rows = attended.transpose(1, 0, 2).reshape(token_count, local_width)
    attn_extended = with_halo(attended_rows, (("ctx", 0),), frame_size)
    attn_grid = padded_grid(attn_extended, frame_count)
    mixed = depthwise(attn_grid, kernel, frame_count, 1).astype(jnp.bfloat16)
    piece = lax.all_gather(grad_rows, "tp", axis=1, tiled=True)
    grad_sum = lax.dot_general(
        piece, point_weight, (((1,), (1,)), ((), ())), preferred_element_type=jnp.float32
    )
    product = lax.dot_general(
        mixed, piece, (((0,), (0,)), ((), ())), preferred_element_type=jnp.float32
    )
    grad_sum, point_columns = (grad_sum, product)
    mixed_grad = grad_sum.astype(jnp.bfloat16)
    grad_grid = mixed_grad.astype(jnp.float32).reshape(frame_count, HH, WW, local_width)
    depth_local = tap_sums(attn_grid, grad_grid, frame_count)
    grad_extended = with_halo(mixed_grad, (("ctx", 0),), frame_size)
    attn_grad = depthwise(padded_grid(grad_extended, frame_count), kernel, frame_count, -1).astype(
        jnp.bfloat16
    )
    grad_scale = 1.0 / math.sqrt(token_count * lax.axis_size("ctx") * lax.axis_size("dp"))
    point_grad, depth_grad = (
        lax.psum((point_columns * grad_scale).astype(jnp.bfloat16), ("ctx", "dp")).astype(
            jnp.float32
        ),
        lax.psum((depth_local * grad_scale).astype(jnp.bfloat16), ("ctx", "dp")).astype(
            jnp.float32
        ),
    )
    grad_heads = attn_grad.reshape(token_count, head_count, HD)
    row_dots = jnp.sum(
        attended_rows.astype(jnp.float32).reshape(token_count, head_count, HD)
        * grad_heads.astype(jnp.float32),
        axis=2,
    ).T
    grad_query, key_terms = key_sweep(
        query_heads,
        grad_heads,
        log_sums,
        row_dots,
        query_blocks,
        key_heads,
        value_heads,
        all_blocks,
        scaling,
    )
    summed = lax.psum_scatter(
        key_terms.astype(jnp.bfloat16), "ctx", scatter_dimension=0, tiled=True
    ).astype(jnp.float32)
    grad_key = summed[:, :local_width]
    grad_value = summed[:, local_width:]
    query_out = grad_query.reshape(token_count, local_width).astype(jnp.bfloat16)[None]
    key_out = grad_key.astype(jnp.bfloat16)[None]
    value_out = grad_value.astype(jnp.bfloat16)[None]
    return (query_out, key_out, value_out, point_grad, depth_grad)


def solution(mesh):
    placed = (
        P("dp", "ctx", "tp"),
        P("dp", "ctx", "tp"),
        P("dp", "ctx", "tp"),
        P("dp", "ctx", "tp"),
        P(None, "tp"),
        P("tp", None),
        P(),
    )
    return jax.shard_map(
        local,
        mesh=mesh,
        in_specs=placed,
        out_specs=(
            P("dp", "ctx", "tp"),
            P("dp", "ctx", "tp"),
            P("dp", "ctx", "tp"),
            P("tp", None),
            P(None, "tp"),
        ),
        check_vma=False,
    )
```

profile of v0, /device:TPU:1, one launch (start us, length us, event | category | flops | bytes accessed | tf_op | source)
XLA Modules:
  0.0 700.9 jit_solution(13415035767248692995)
XLA Ops:
  15.2 26.2 %all-gather.11.cloned.1.call-done = bf16[1,256,3072]{2,1,0:T(8,128)(2,1)} async-done(((bf16[1,256,384]{2,1,0:T(8,128)(2,1)}), bf16[1,256,3072]{2,1,0:T(8,128)(2,1)}) %all-gather.11.cloned.1.call-update) | async-done | bytes 1572880 | tf_op jit(solution)/shard_map/all_gather | solution.py:231
  41.4 2.4 fusion.25
  45.1 5.5 collective-permute-start
  51.4 2.5 collective-permute-done
  57.1 78.9 %all-gather.7.cloned.1.call-done = bf16[1,4096,384]{1,2,0:T(8,128)(2,1)} async-done(((bf16[1,256,384]{1,2,0:T(8,128)(2,1)}), bf16[1,4096,384]{1,2,0:T(8,128)(2,1)}) %all-gather.7.cloned.1.call-update) | async-done | bytes 3145744 | tf_op jit(solution)/shard_map/all_gather | solution.py:216
  136.0 4.6 copy.96
  140.6 90.1 %all-gather.9.cloned.1.call-done = bf16[1,4096,384]{1,2,0:T(8,128)(2,1)} async-done(((bf16[1,256,384]{1,2,0:T(8,128)(2,1)}), bf16[1,4096,384]{1,2,0:T(8,128)(2,1)}) %all-gather.9.cloned.1.call-update) | async-done | bytes 3145744 | tf_op jit(solution)/shard_map/all_gather | solution.py:217
  230.8 4.7 copy.93
  235.4 55.4 %while.34 = (s32[]{:T(128)}, f32[3,256]{1,0:T(4,128)S(1)}, f32[3,256]{1,0:T(4,128)S(1)}, f32[3,256,128]{2,1,0:T(8,128)S(1)}, s32[4096]{0:T(1024)}, /*index=5*/s3...) while((s32[]{:T(128)}, f32[3,256]{1,0:T(4,128)S(1)}, ...), condition=%wide.region_5.6_spmd.clone, body=%wide.region_2.5_spmd.clone.sunk | while | flops 204508928 | bytes 13098215 | solution.py:146
  236.4 2.6 fusion.122
  243.3 2.6 fusion.122
  250.2 2.6 fusion.122
  257.1 2.6 fusion.122
  264.1 2.6 fusion.122
  271.0 2.6 fusion.122
  277.9 2.6 fusion.122
  284.9 2.6 fusion.122
  299.6 6.1 collective-permute-start.2
  312.5 2.3 multiply_convert_fusion
  315.1 3.1 broadcast_in_dim.132.clone
  318.1 90.6 %while.35 = (s32[]{:T(128)}, f32[256,3,128]{0,2,1:T(8,128)}, bf16[4096,768]{1,0:T(8,128)(2,1)}, bf16[4096,3,128]{2,0,1:T(8,128)(2,1)}, s32[4096]{0:T(1024)}, /*i...) while((s32[]{:T(128)}, f32[256,3,128]{0,2,1:T(8,128)}, ...), condition=%wide.region_8.9_spmd.clone, body=%wide.region_7.8_spmd.clone.sunk | while | flops 508461056 | bytes 28194072 | solution.py:199
  334.3 2.3 fusion.137
  345.6 2.3 fusion.137
  357.0 2.3 fusion.137
  368.3 2.3 fusion.137
  379.6 2.3 fusion.137
  390.9 2.3 fusion.137
  402.3 2.3 fusion.137
  410.5 2.4 multiply_reduce_fusion.21
  414.1 113.5 %psum.15 = bf16[27,384]{1,0:T(8,128)(2,1)S(1)} all-reduce(bf16[27,384]{1,0:T(8,128)(2,1)S(1)} %multiply_convert_fusion.1), channel_id=1, replica_groups=mesh['ctx'=16,'tp'=8,'dp'=2] {'ctx','dp'}, use_global_device_ids=true, to_apply=%region_38.39 | all-reduce | flops 10368 | bytes 41472 | tf_op jit(solution)/shard_map/psum | solution.py:251
  528.2 4.5 convert_element_type.118
  532.7 159.8 %reduce-scatter.2.cloned.1.call-done = bf16[256,768]{1,0:T(8,128)(2,1)} async-done(((bf16[4096,768]{1,0:T(8,128)(2,1)}), bf16[256,768]{1,0:T(8,128)(2,1)}) %reduce-scatter.2.cloned.1.call-update) | async-done | bytes 393232 | tf_op jit(solution)/shard_map/reduce_scatter | solution.py:272
  (399 shorter events, 141.7 us)
Async XLA Ops:
  7.2 34.2 %all-gather.11.cloned.1.call-start = ((), (), s32[]{:S(2)}) async-start(), calls=%async_computation.5 | async-start | bytes 1769472 | tf_op jit(solution)/shard_map/all_gather | solution.py:231
  7.9 128.1 %all-gather.7.cloned.1.call-start = ((), (), s32[]{:S(2)}) async-start(), calls=%async_computation.3 | async-start | bytes 3342336 | tf_op jit(solution)/shard_map/all_gather | solution.py:216
  9.8 221.0 %all-gather.9.cloned.1.call-start = ((), (), s32[]{:S(2)}) async-start(), calls=%async_computation.4 | async-start | bytes 3342336 | tf_op jit(solution)/shard_map/all_gather | solution.py:217
  11.6 516.7 %all-reduce.4.cloned.1.call-start = ((), (), s32[]{:S(2)}) async-start(), calls=%async_computation.2 | async-start | bytes 4718592 | tf_op jit(solution)/shard_map/psum | solution.py:248
  13.5 40.5 %copy-start.12 = (f32[384]{0:T(512)}, f32[384]{0:T(512)S(1)}, u32[]{:S(2)}) copy-start(f32[384]{0:T(512)S(1)} %get-tuple-element.548) | copy-start | bytes 4612
  13.6 40.5 %copy-start.14 = (f32[384]{0:T(512)}, f32[384]{0:T(512)S(1)}, u32[]{:S(2)}) copy-start(f32[384]{0:T(512)S(1)} %get-tuple-element.549) | copy-start | bytes 4612
  13.6 40.5 %copy-start.16 = (f32[384]{0:T(512)}, f32[384]{0:T(512)S(1)}, u32[]{:S(2)}) copy-start(f32[384]{0:T(512)S(1)} %get-tuple-element.550) | copy-start | bytes 4612
  13.6 40.5 %copy-start.18 = (f32[384]{0:T(512)}, f32[384]{0:T(512)S(1)}, u32[]{:S(2)}) copy-start(f32[384]{0:T(512)S(1)} %get-tuple-element.551) | copy-start | bytes 4612
  13.6 40.5 %copy-start.20 = (f32[384]{0:T(512)}, f32[384]{0:T(512)S(1)}, u32[]{:S(2)}) copy-start(f32[384]{0:T(512)S(1)} %get-tuple-element.552) | copy-start | bytes 4612
  13.6 40.5 %copy-start.22 = (f32[384]{0:T(512)}, f32[384]{0:T(512)S(1)}, u32[]{:S(2)}) copy-start(f32[384]{0:T(512)S(1)} %get-tuple-element.553) | copy-start | bytes 4612
  13.6 40.5 %copy-start.24 = (f32[384]{0:T(512)}, f32[384]{0:T(512)S(1)}, u32[]{:S(2)}) copy-start(f32[384]{0:T(512)S(1)} %get-tuple-element.554) | copy-start | bytes 4612
  14.3 39.8 %copy-start.28 = (f32[384]{0:T(512)}, f32[384]{0:T(512)S(1)}, u32[]{:S(2)}) copy-start(f32[384]{0:T(512)S(1)} %get-tuple-element.529) | copy-start | bytes 4612
  14.3 39.8 %copy-start.30 = (f32[384]{0:T(512)}, f32[384]{0:T(512)S(1)}, u32[]{:S(2)}) copy-start(f32[384]{0:T(512)S(1)} %get-tuple-element.530) | copy-start | bytes 4612
  14.3 39.8 %copy-start.32 = (f32[384]{0:T(512)}, f32[384]{0:T(512)S(1)}, u32[]{:S(2)}) copy-start(f32[384]{0:T(512)S(1)} %get-tuple-element.531) | copy-start | bytes 4612
  14.3 39.8 %copy-start.34 = (f32[384]{0:T(512)}, f32[384]{0:T(512)S(1)}, u32[]{:S(2)}) copy-start(f32[384]{0:T(512)S(1)} %get-tuple-element.532) | copy-start | bytes 4612
  14.3 39.8 %copy-start.36 = (f32[384]{0:T(512)}, f32[384]{0:T(512)S(1)}, u32[]{:S(2)}) copy-start(f32[384]{0:T(512)S(1)} %get-tuple-element.533) | copy-start | bytes 4612
  14.3 39.8 %copy-start.38 = (f32[384]{0:T(512)}, f32[384]{0:T(512)S(1)}, u32[]{:S(2)}) copy-start(f32[384]{0:T(512)S(1)} %get-tuple-element.534) | copy-start | bytes 4612
  14.3 39.8 %copy-start.40 = (f32[384]{0:T(512)}, f32[384]{0:T(512)S(1)}, u32[]{:S(2)}) copy-start(f32[384]{0:T(512)S(1)} %get-tuple-element.535) | copy-start | bytes 4612
  14.4 39.8 %copy-start.42 = (f32[384]{0:T(512)}, f32[384]{0:T(512)S(1)}, u32[]{:S(2)}) copy-start(f32[384]{0:T(512)S(1)} %get-tuple-element.536) | copy-start | bytes 4612
  14.4 39.8 %copy-start.44 = (f32[384]{0:T(512)}, f32[384]{0:T(512)S(1)}, u32[]{:S(2)}) copy-start(f32[384]{0:T(512)S(1)} %get-tuple-element.537) | copy-start | bytes 4612
  14.4 39.8 %copy-start.46 = (f32[384]{0:T(512)}, f32[384]{0:T(512)S(1)}, u32[]{:S(2)}) copy-start(f32[384]{0:T(512)S(1)} %get-tuple-element.538) | copy-start | bytes 4612
  14.4 39.8 %copy-start.48 = (f32[384]{0:T(512)}, f32[384]{0:T(512)S(1)}, u32[]{:S(2)}) copy-start(f32[384]{0:T(512)S(1)} %get-tuple-element.539) | copy-start | bytes 4612
  14.4 39.8 %copy-start.50 = (f32[384]{0:T(512)}, f32[384]{0:T(512)S(1)}, u32[]{:S(2)}) copy-start(f32[384]{0:T(512)S(1)} %get-tuple-element.540) | copy-start | bytes 4612
  14.4 39.8 %copy-start.52 = (f32[384]{0:T(512)}, f32[384]{0:T(512)S(1)}, u32[]{:S(2)}) copy-start(f32[384]{0:T(512)S(1)} %get-tuple-element.541) | copy-start | bytes 4612
  14.4 39.8 %copy-start.54 = (f32[384]{0:T(512)}, f32[384]{0:T(512)S(1)}, u32[]{:S(2)}) copy-start(f32[384]{0:T(512)S(1)} %get-tuple-element.542) | copy-start | bytes 4612
  14.4 39.8 %copy-start.56 = (f32[384]{0:T(512)}, f32[384]{0:T(512)S(1)}, u32[]{:S(2)}) copy-start(f32[384]{0:T(512)S(1)} %get-tuple-element.543) | copy-start | bytes 4612
  14.4 39.8 %copy-start.58 = (f32[384]{0:T(512)}, f32[384]{0:T(512)S(1)}, u32[]{:S(2)}) copy-start(f32[384]{0:T(512)S(1)} %get-tuple-element.544) | copy-start | bytes 4612
  43.8 7.5 %collective-permute-start.1 = (bf16[128,384]{1,0:T(8,128)(2,1)S(1)}, bf16[128,384]{1,0:T(8,128)(2,1)S(1)}, u32[]{:S(2)}, u32[]{:S(2)}) collective-permute-start(bf16[128,384]{1,0:T(8,128)(2,1)S(1)} %get-tuple-element.614), channel_id=1, source_target_pairs={{16,0},{32,16},{48,32},{64,48},{80,64},{96,80},{112,96},{128,112},... | collective-permute-start | bytes 294920 | tf_op jit(solution)/shard_map/ppermute | solution.py:26
  45.1 8.7 %collective-permute-start = (bf16[128,384]{1,0:T(8,128)(2,1)S(1)}, bf16[128,384]{1,0:T(8,128)(2,1)S(1)}, u32[]{:S(2)}, u32[]{:S(2)}) collective-permute-start(bf16[128,384]{1,0:T(8,128)(2,1)S(1)} %get-tuple-element.613), channel_id=1, source_target_pairs={{0,16},{16,32},{32,48},{48,64},{64,80},{80,96},{96,112},{112,128},... | collective-permute-start | bytes 294920 | tf_op jit(solution)/shard_map/ppermute | solution.py:24
  295.9 12.5 %collective-permute-start.3 = (bf16[128,384]{1,0:T(8,128)(2,1)}, bf16[128,384]{1,0:T(8,128)(2,1)}, u32[]{:S(2)}, u32[]{:S(2)}) collective-permute-start(bf16[128,384]{1,0:T(8,128)(2,1)} %copy.105), channel_id=1, source_target_pairs={{16,0},{32,16},{48,32},{64,48},{80,64},{96,80},{112,96},{128,112},... | collective-permute-start | bytes 294920 | tf_op jit(solution)/shard_map/ppermute | solution.py:26
  299.6 8.8 %collective-permute-start.2 = (bf16[128,384]{1,0:T(8,128)(2,1)}, bf16[128,384]{1,0:T(8,128)(2,1)}, u32[]{:S(2)}, u32[]{:S(2)}) collective-permute-start(bf16[128,384]{1,0:T(8,128)(2,1)} %copy.102), channel_id=1, source_target_pairs={{0,16},{16,32},{32,48},{48,64},{64,80},{80,96},{96,112},{112,128},... | collective-permute-start | bytes 294920 | tf_op jit(solution)/shard_map/ppermute | solution.py:24
  314.8 377.7 %reduce-scatter.2.cloned.1.call-start = ((), (), s32[]{:S(2)}) async-start(), calls=%async_computation.1 | async-start | bytes 6684672 | tf_op jit(solution)/shard_map/reduce_scatter | solution.py:272
  (69 other events, 214.6 us)
Sparse Core Ops, SparseCore 0:
  9.9 31.4 all-gather.10
  44.4 91.5 all-gather.6
  139.1 91.6 all-gather.8
  314.9 155.1 all-reduce.3
  474.7 217.7 reduce-scatter.1
where the time goes:
time: 707 us; the launch traced here: 701 us
  waiting for transfers between devices  359 us (51%)
  blocking collectives  113 us (16%)
  matrix products  85.1 us (12%)
  local copies, waits for them, and re-layouts  73.4 us (10%)
  other arithmetic  39.6 us (6%)
  between operations  14.9 us (2%)
  starting transfers between devices  14.6 us (2%)
    reduce_scatter x1, waiting for transfers between devices, local(): lax.psum_scatter(key_terms.astype(jnp.bfloat16), 'ctx', scatter_dimension...  160 us
    psum x1, blocking collectives, local(): lax.psum((depth_local * grad_scale).astype(jnp.bfloat16), ('ctx', 'dp'))  113 us
    all_gather x1, waiting for transfers between devices, local(): lax.all_gather(value_rows, 'ctx', axis=0, tiled=True)  90.1 us
    all_gather x1, waiting for transfers between devices, local(): lax.all_gather(key_rows, 'ctx', axis=0, tiled=True)  78.9 us
    dot_general x16, matrix products, masked_scores(): jnp.einsum('qhd,khd->hqk', query_heads, key_heads, preferred_element_type...  32.7 us
    all_gather x1, waiting for transfers between devices, local(): piece = lax.all_gather(grad_rows, 'tp', axis=1, tiled=True)  26.2 us
    dynamic_update_slice x16, local copies, waits for them, and re-layouts, key_step(): key_terms = lax.dynamic_update_slice_in_dim(key_terms, joined, first_row, 0)  18.9 us
    dot_general x8, matrix products, grad_tile(): jnp.einsum('hqk,khd->qhd', dscores, key_heads, preferred_element_type=jnp...  18.4 us
  transfers between devices with their start and end apart: 9, of which 6 were waited for; matrix products, arithmetic and copies ran while one was open for 16% of the time, Pallas kernels for 0%

commit v1 on v0

v1 whole, which is shorter than its diff:
```python
import math

import jax
import jax.numpy as jnp
from jax import lax
from jax.experimental import pallas as pl
from jax.experimental.pallas import tpu as pltpu
from jax.sharding import PartitionSpec as P

HD = 128
HH = 8
WW = 16
FRAME = HH * WW
NEG = -1e30
OPEN = 3e38
MESH = pl.DeviceIdType.MESH
F32 = jnp.float32
BF16 = jnp.bfloat16

ZN = 8
XN = 4
TN = 8
CN = 16
ROWS = 256
COLS = 384
HEADS = COLS // HD
PIECE = COLS // ZN


def wait(ref, sem):
    pltpu.make_async_copy(ref, ref, sem).wait()


def nt(a, b):
    return lax.dot_general(a, b, (((1,), (1,)), ((), ())), preferred_element_type=F32)


def nn(a, b):
    return lax.dot_general(a, b, (((1,), (0,)), ((), ())), preferred_element_type=F32)


def tn(a, b):
    return lax.dot_general(a, b, (((0,), (0,)), ((), ())), preferred_element_type=F32)


def spread_columns(shifted, plain):
    column = lax.broadcasted_iota(jnp.int32, (FRAME, COLS), 0) % WW
    for frame in range(4):
        cells = plain[frame].astype(F32)
        shifted[1, frame, WW : WW + FRAME] = cells
        shifted[0, frame, WW : WW + FRAME] = jnp.where(
            column > 0, pltpu.roll(cells, 1, 0), 0.0
        )
        shifted[2, frame, WW : WW + FRAME] = jnp.where(
            column < WW - 1, pltpu.roll(cells, FRAME - 1, 0), 0.0
        )


def body(
    q_in, k_in, v_in, g_in, w_ref, kern_in, bound_ref,
    dq_out, dk_out, dv_out, point_out, depth_out,
    q, kv, og, kern, row_max, row_sum, acc, lse, dots,
    mg_send, mg_ext, at_ext, shifted, mixed, mixed_own, dsum, dsum_own,
    do, dq_acc, terms, xsend, xrecv, sbuf, rbuf,
    prod, xr, relay, qsum, zr, allq, dx, dz, fin, finr,
    swap_s, swap_r, og_s, og_r, ring_s, ring_r, sib_s, sib_r, halo_s, halo_r,
    bs_s, bs_r, bx_s, bx_r, px_s, px_r, pz_s, pz_r, gz_s, gz_r, gx_s, gx_r,
    dx_s, dx_r, dz_s, dz_r,
):
    ctx, tp, dp = lax.axis_index("ctx"), lax.axis_index("tp"), lax.axis_index("dp")
    z, half = ctx // 2, ctx % 2
    y, core = tp // 2, tp % 2
    chunk = 2 * z + core
    xi = 2 * half + dp
    off = half != core
    same = half == core
    scaling = 1.0 / math.sqrt(HD)
    factor = scaling * math.log2(math.e)

    def at_z(step):
        return (2 * lax.rem(z + step + ZN, ZN) + half, tp, dp)

    def at_x(step):
        place = lax.rem(xi + step + XN, XN)
        return (2 * z + place // 2, tp, lax.rem(place, 2))

    def at_tp(step):
        return (ctx, lax.rem(tp + step, TN), dp)

    sibling = (ctx, 2 * y + 1 - core, dp)
    partner = (2 * z + 1 - half, 2 * y + 1 - core, dp)
    below = lax.rem(z + ZN - 1 + core, ZN)
    above = lax.rem(z + core, ZN)
    prev_dev = (2 * below + half, 2 * y + 1 - core, dp)
    next_dev = (2 * above + half, 2 * y + 1 - core, dp)
    other = lax.rem(z + ZN - 1 + 2 * core, ZN)
    halo_dev = (2 * other + half, 2 * y + 1 - core, dp)

    barrier = pltpu.get_barrier_semaphore()
    peers = [at_tp(i) for i in range(1, TN)]
    peers += [at_z(i) for i in range(1, ZN)]
    peers += [at_x(i) for i in range(1, XN)]
    peers += [partner, halo_dev]
    for device in peers:
        pl.semaphore_signal(barrier, inc=1, device_id=device, device_id_type=MESH)
    pl.semaphore_wait(barrier, len(peers))

    def send(src, dst, send_sem, recv_sem, device):
        pltpu.make_async_remote_copy(
            src_ref=src, dst_ref=dst, send_sem=send_sem, recv_sem=recv_sem,
            device_id=device, device_id_type=MESH,
        ).start()

    def swap(i, src, dst):
        @pl.when(off)
        def _():
            send(src, dst, swap_s.at[i], swap_r.at[i], partner)

        @pl.when(same)
        def _():
            pltpu.make_async_copy(src, dst, swap_r.at[i]).start()

    swap(0, k_in, kv.at[0, ctx])
    swap(1, v_in, kv.at[1, ctx])
    swap(2, q_in, q)
    swap(3, kern_in, kern)
    for i in range(1, TN):
        send(g_in, og.at[tp], og_s.at[i], og_r.at[i], at_tp(i))
    keep = pltpu.make_async_copy(g_in, og.at[tp], og_r.at[0])
    keep.start()

    acc[...] = jnp.zeros_like(acc)
    row_sum[...] = jnp.zeros_like(row_sum)
    row_max[...] = jnp.full_like(row_max, NEG)
    dq_acc[...] = jnp.zeros_like(dq_acc)
    shifted[...] = jnp.zeros_like(shifted)
    rbuf[0, 3, 1] = jnp.zeros((ROWS, COLS), BF16)
    rbuf[1, 3, 0] = jnp.zeros((ROWS, COLS), BF16)

    def ring(direction, distance, part, source):
        place = kv.at[part, source]
        send(
            place, place, ring_s.at[direction, distance - 1, part],
            ring_r.at[direction, distance - 1, part], at_z(1 if direction == 0 else -1),
        )

    def ring_wait(direction, distance, part, source):
        wait(kv.at[part, source], ring_r.at[direction, distance - 1, part])

    def to_sibling(slot, source):
        send(kv.at[:, source], kv.at[:, source], sib_s.at[slot], sib_r.at[slot], sibling)

    for part in range(2):
        wait(kv.at[part, chunk], swap_r.at[part])
        ring(0, 1, part, chunk)
        ring(1, 1, part, chunk)
    to_sibling(0, chunk)

    def flip(index):
        return index + 1 - 2 * lax.rem(index, 2)

    def fwd_chunk(index):
        @pl.when(index <= chunk + 2)
        def _():
            limits = bound_ref[index]
            for head in range(HEADS):
                lanes = slice(head * HD, (head + 1) * HD)
                keys = kv[0, index, :, lanes]
                vals = kv[1, index, :, lanes]
                scores = nt(keys, q[:, lanes])
                scores = jnp.concatenate(
                    [
                        jnp.minimum(scores[:FRAME], limits[0:1]),
                        jnp.minimum(scores[FRAME:], limits[1:2]),
                    ],
                    axis=0,
                )
                old = row_max[head]
                new = jnp.maximum(old, jnp.max(scores, axis=0, keepdims=True))
                weights = jnp.exp2(scores * factor - new * factor)
                shrink = jnp.exp2((old - new) * factor)
                row_max[head] = new
                row_sum[head] = row_sum[head] * shrink + jnp.sum(weights, axis=0, keepdims=True)
                acc[head] = acc[head] * shrink + tn(vals, weights.astype(BF16))

    wait(q, swap_r.at[2])

    def near(i, carry):
        @pl.when(i == 1)
        def _():
            wait(kv.at[:, flip(chunk)], sib_r.at[0])

        fwd_chunk(jnp.where(i == 0, chunk, flip(chunk)))
        return carry

    lax.fori_loop(0, 2, near, 0)

    def fwd_step(distance):
        low = 2 * lax.rem(z - distance + ZN, ZN) + core
        high = 2 * lax.rem(z + distance, ZN) + core
        for part in range(2):
            ring_wait(0, distance, part, low)
            if distance < 3 or part == 0:
                ring(0, distance + 1, part, low)
            ring_wait(1, distance, part, high)
            if distance < 3 or part == 1:
                ring(1, distance + 1, part, high)
        to_sibling(distance, low)
        to_sibling(3 + distance, high)

        def step(i, carry):
            @pl.when(i == 2)
            def _():
                wait(kv.at[:, flip(low)], sib_r.at[distance])
                wait(kv.at[:, flip(high)], sib_r.at[3 + distance])

            index = jnp.where(lax.rem(i, 2) == 0, low, high)
            fwd_chunk(jnp.where(i < 2, index, flip(index)))
            return carry

        lax.fori_loop(0, 4, step, 0)

    fwd_step(1)

    keep.wait()
    for i in range(1, TN):
        wait(og.at[lax.rem(tp + TN - i, TN)], og_r.at[i])
    total = nt(og[0], w_ref[:, 0:COLS])
    for i in range(1, TN):
        total += nt(og[i], w_ref[:, i * COLS : (i + 1) * COLS])
    mg_send[...] = total.astype(BF16).reshape(2, FRAME, COLS)
    swap(4, mg_send, mg_ext.at[1:3])

    fwd_step(2)

    def halo(which, ext):
        @pl.when(chunk > 0)
        def _():
            send(ext.at[1], ext.at[3], halo_s.at[which, 0], halo_r.at[which, 0], prev_dev)

        @pl.when(chunk < CN - 1)
        def _():
            send(ext.at[2], ext.at[0], halo_s.at[which, 1], halo_r.at[which, 1], next_dev)

        @pl.when(chunk == 0)
        def _():
            ext[0] = jnp.zeros((FRAME, COLS), BF16)

        @pl.when(chunk == CN - 1)
        def _():
            ext[3] = jnp.zeros((FRAME, COLS), BF16)

    def halo_wait(which, ext):
        @pl.when(chunk > 0)
        def _():
            wait(ext.at[1], halo_s.at[which, 0])
            wait(ext.at[0], halo_r.at[which, 1])

        @pl.when(chunk < CN - 1)
        def _():
            wait(ext.at[2], halo_s.at[which, 1])
            wait(ext.at[3], halo_r.at[which, 0])

    wait(mg_ext.at[1:3], swap_r.at[4])
    halo(0, mg_ext)

    fwd_step(3)

    last = 2 * lax.rem(z + 4, ZN) + core
    ring_wait(0, 4, 0, last)
    ring_wait(1, 4, 1, last)
    to_sibling(7, last)

    def far(i, carry):
        @pl.when(i == 1)
        def _():
            wait(kv.at[:, flip(last)], sib_r.at[7])

        fwd_chunk(jnp.where(i == 0, last, flip(last)))
        return carry

    lax.fori_loop(0, 2, far, 0)

    for head in range(HEADS):
        lanes = slice(head * HD, (head + 1) * HD)
        sums = row_sum[head]
        lse[head] = row_max[head] * factor + jnp.log(sums) * math.log2(math.e)
        rows = jnp.transpose(acc[head] / sums).astype(BF16)
        at_ext[1, :, lanes] = rows[:FRAME]
        at_ext[2, :, lanes] = rows[FRAME:]
    halo(1, at_ext)

    wait(kern, swap_r.at[3])
    halo_wait(0, mg_ext)
    spread_columns(shifted, mg_ext)

    def taps():
        return [(a, r, c) for a in (-1, 0, 1) for r in (-1, 0, 1) for c in (-1, 0, 1)]

    for frame in range(2):
        for head in range(HEADS):
            lanes = slice(head * HD, (head + 1) * HD)
            result = jnp.zeros((FRAME, HD), F32)
            for tap, (a, r, c) in enumerate(taps()):
                first = WW - WW * r
                window = shifted[1 - c, frame + 1 - a, first : first + FRAME, lanes]
                result = result + kern[tap : tap + 1, lanes] * window
            do[frame * FRAME : (frame + 1) * FRAME, lanes] = result.astype(BF16)

    halo_wait(1, at_ext)
    for head in range(HEADS):
        lanes = slice(head * HD, (head + 1) * HD)
        attended = jnp.concatenate([at_ext[1, :, lanes], at_ext[2, :, lanes]], axis=0)
        product = attended.astype(F32) * do[:, lanes].astype(F32)
        dots[head] = jnp.sum(jnp.transpose(product), axis=0, keepdims=True)

    spread_columns(shifted, at_ext)
    dsum[...] = jnp.zeros_like(dsum)
    grad_scale = 1.0 / math.sqrt(2.0 * CN * ROWS)
    for frame in range(2):
        for head in range(HEADS):
            lanes = slice(head * HD, (head + 1) * HD)
            result = jnp.zeros((FRAME, HD), F32)
            grad = mg_ext[1 + frame, :, lanes].astype(F32)
            for tap, (a, r, c) in enumerate(taps()):
                first = WW + WW * r
                window = shifted[1 + c, frame + 1 + a, first : first + FRAME, lanes]
                result = result + kern[tap : tap + 1, lanes] * window
                dsum[tap : tap + 1, lanes] += (
                    jnp.sum(window * grad, axis=0, keepdims=True) * grad_scale
                )
            mixed[frame * FRAME : (frame + 1) * FRAME, lanes] = result.astype(BF16)
    swap(5, mixed, mixed_own)
    swap(6, dsum, dsum_own)

    def bwd_chunk(index):
        @pl.when(index > chunk + 2)
        def _():
            terms[...] = jnp.zeros_like(terms)

        @pl.when(index <= chunk + 2)
        def _():
            limits = bound_ref[index]
            for head in range(HEADS):
                lanes = slice(head * HD, (head + 1) * HD)
                keys = kv[0, index, :, lanes]
                vals = kv[1, index, :, lanes]
                queries = q[:, lanes]
                grads = do[:, lanes]
                scores = nt(keys, queries)
                scores = jnp.concatenate(
                    [
                        jnp.minimum(scores[:FRAME], limits[0:1]),
                        jnp.minimum(scores[FRAME:], limits[1:2]),
                    ],
                    axis=0,
                )
                probs = jnp.exp2(scores * factor - lse[head])
                dscores = (probs * (nt(vals, grads) - dots[head])).astype(BF16)
                terms[1, :, lanes] = nn(probs.astype(BF16), grads)
                terms[0, :, lanes] = nn(dscores, queries) * scaling
                dq_acc[head] = dq_acc[head] + tn(keys, dscores)

    def share(slot):
        xsend[slot] = terms[...].astype(BF16)
        send(xsend.at[slot], xrecv.at[slot], bx_s.at[slot], bx_r.at[slot], sibling)

    def shared(slot):
        wait(xrecv.at[slot], bx_r.at[slot])
        return terms[...] + xrecv[slot].astype(F32)

    target = 2 * lax.rem(z + 4, ZN) + core

    def bwd_far(i, carry):
        bwd_chunk(jnp.where(i == 0, flip(target), target))

        @pl.when(i == 0)
        def _():
            share(7)

        return carry

    lax.fori_loop(0, 2, bwd_far, 0)
    total = shared(7).astype(BF16)
    sbuf[0, 3, 0] = total[0]
    sbuf[1, 3, 1] = total[1]
    send(sbuf.at[0, 3, 0], rbuf.at[0, 3, 0], bs_s.at[0, 3], bs_r.at[0, 3], at_z(1))
    send(sbuf.at[1, 3, 1], rbuf.at[1, 3, 1], bs_s.at[1, 3], bs_r.at[1, 3], at_z(-1))

    def bwd_step(distance):
        up = 2 * lax.rem(z + distance, ZN) + core
        down = 2 * lax.rem(z - distance + ZN, ZN) + core

        def step(i, carry):
            side = lax.rem(i, 2)
            index = jnp.where(side == 0, up, down)
            bwd_chunk(jnp.where(i < 2, flip(index), index))
            slot = distance + 3 * side

            @pl.when(i < 2)
            def _():
                share(slot)

            @pl.when(i >= 2)
            def _():
                if distance == 3:
                    wait(rbuf.at[side, 3, side], bs_r.at[side, 3])
                else:
                    wait(rbuf.at[side, distance], bs_r.at[side, distance])
                added = shared(slot) + rbuf[side, distance].astype(F32)
                sbuf[side, distance - 1] = added.astype(BF16)
                goal = lax.rem(z + ZN + 1 - 2 * side, ZN)
                send(
                    sbuf.at[side, distance - 1], rbuf.at[side, distance - 1],
                    bs_s.at[side, distance - 1], bs_r.at[side, distance - 1],
                    (2 * goal + half, tp, dp),
                )

            return carry

        lax.fori_loop(0, 4, step, 0)

    wait(mixed_own, swap_r.at[5])

    def product(i, carry):
        block = tn(mixed_own[...], og[i]) * grad_scale
        prod[i // 2, lax.rem(i, 2)] = block.astype(BF16).reshape(ZN, PIECE, COLS)
        return carry

    lax.fori_loop(0, TN, product, 0)
    across = lax.rem(xi + 2, XN)
    right = lax.rem(xi + 1, XN)
    left = lax.rem(xi + 3, XN)
    lower, upper = slice(0, ZN // 2), slice(ZN // 2, ZN)
    send(prod.at[across, :, lower], xr.at[0, 0], px_s.at[0, 0], px_r.at[0, 0], at_x(1))
    send(prod.at[across, :, upper], xr.at[1, 0], px_s.at[1, 0], px_r.at[1, 0], at_x(-1))
    send(prod.at[right, :, upper], xr.at[0, 1], px_s.at[0, 1], px_r.at[0, 1], at_x(1))
    send(prod.at[left, :, lower], xr.at[1, 1], px_s.at[1, 1], px_r.at[1, 1], at_x(-1))
    wait(dsum_own, swap_r.at[6])
    for i in range(1, XN):
        send(dsum_own, dx.at[i], dx_s.at[i], dx_r.at[i], at_x(i))

    bwd_step(3)

    wait(xr.at[0, 0], px_r.at[0, 0])
    relay[0] = (prod[right, :, lower].astype(F32) + xr[0, 0].astype(F32)).astype(BF16)
    send(relay.at[0], xr.at[0, 2], px_s.at[0, 2], px_r.at[0, 2], at_x(1))
    wait(xr.at[1, 0], px_r.at[1, 0])
    relay[1] = (prod[left, :, upper].astype(F32) + xr[1, 0].astype(F32)).astype(BF16)
    send(relay.at[1], xr.at[1, 2], px_s.at[1, 2], px_r.at[1, 2], at_x(-1))
    sums = dsum_own[...]
    for i in range(1, XN):
        wait(dx.at[i], dx_r.at[i])
        sums = sums + dx[i]
    dz[0] = sums
    for i in range(1, ZN):
        send(dz.at[0], dz.at[i], dz_s.at[i], dz_r.at[i], at_z(i))

    bwd_step(2)

    for side in range(2):
        for slot in (1, 2):
            wait(xr.at[side, slot], px_r.at[side, slot])
    qsum[:, lower] = (
        prod[xi, :, lower].astype(F32) + xr[0, 2].astype(F32) + xr[1, 1].astype(F32)
    ).astype(BF16)
    qsum[:, upper] = (
        prod[xi, :, upper].astype(F32) + xr[0, 1].astype(F32) + xr[1, 2].astype(F32)
    ).astype(BF16)
    for i in range(1, ZN):
        goal = lax.rem(z + i, ZN)
        send(qsum.at[:, goal], zr.at[i], pz_s.at[i], pz_r.at[i], at_z(i))

    bwd_step(1)

    piece = qsum[:, z].astype(F32)
    for i in range(1, ZN):
        wait(zr.at[i], pz_r.at[i])
        piece = piece + zr[i].astype(F32)
    allq[xi, :, z] = piece.astype(BF16)
    for i in range(1, ZN):
        send(allq.at[xi, :, z], allq.at[xi, :, z], gz_s.at[i], gz_r.at[i], at_z(i))

    def bwd_own(i, carry):
        bwd_chunk(jnp.where(i == 0, flip(chunk), chunk))

        @pl.when(i == 0)
        def _():
            share(0)

        return carry

    lax.fori_loop(0, 2, bwd_own, 0)
    for head in range(HEADS):
        lanes = slice(head * HD, (head + 1) * HD)
        fin[0, :, lanes] = (jnp.transpose(dq_acc[head]) * scaling).astype(BF16)
    swap(7, fin.at[0], finr.at[0])
    total = shared(0)
    for side in range(2):
        wait(rbuf.at[side, 0], bs_r.at[side, 0])
        total = total + rbuf[side, 0].astype(F32)
    fin[1:3] = total.astype(BF16)
    swap(8, fin.at[1:3], finr.at[1:3])

    for i in range(1, ZN):
        goal = lax.rem(z + ZN - i, ZN)
        wait(allq.at[xi, :, goal], gz_r.at[i])
    send(allq.at[xi], allq.at[xi], gx_s.at[0, 0], gx_r.at[0, 0], at_x(1))
    send(allq.at[xi], allq.at[xi], gx_s.at[1, 0], gx_r.at[1, 0], at_x(-1))

    sums = dz[0]
    for i in range(1, ZN):
        wait(dz.at[i], dz_r.at[i])
        sums = sums + dz[i]
    depth_out[...] = sums

    def put(quarter):
        for block in range(2):
            cells = allq[quarter, block].reshape(COLS, COLS).astype(F32)
            first = pl.multiple_of((2 * quarter + block) * COLS, HD)
            point_out[:, pl.ds(first, COLS)] = cells

    put(xi)
    wait(allq.at[left], gx_r.at[0, 0])
    send(
        allq.at[left, :, lower], allq.at[left, :, lower], gx_s.at[0, 1], gx_r.at[0, 1], at_x(1)
    )
    wait(allq.at[right], gx_r.at[1, 0])
    send(
        allq.at[right, :, upper], allq.at[right, :, upper], gx_s.at[1, 1], gx_r.at[1, 1],
        at_x(-1),
    )
    put(left)
    put(right)
    wait(finr.at[0], swap_r.at[7])
    dq_out[...] = finr[0]
    wait(finr.at[1:3], swap_r.at[8])
    dk_out[...] = finr[1]
    dv_out[...] = finr[2]
    wait(allq.at[across, :, lower], gx_r.at[0, 1])
    wait(allq.at[across, :, upper], gx_r.at[1, 1])
    put(across)

    @pl.when(off)
    def _():
        wait(k_in, swap_s.at[0])
        wait(v_in, swap_s.at[1])
        wait(q_in, swap_s.at[2])
        wait(kern_in, swap_s.at[3])
        wait(mg_send, swap_s.at[4])
        wait(mixed, swap_s.at[5])
        wait(dsum, swap_s.at[6])
        wait(fin.at[0], swap_s.at[7])
        wait(fin.at[1:3], swap_s.at[8])

    for i in range(1, TN):
        wait(g_in, og_s.at[i])
    for direction in range(2):
        for distance in range(1, 5):
            for part in range(2):
                if distance < 4 or part == direction:
                    wait(kv.at[part, chunk], ring_s.at[direction, distance - 1, part])
            if distance < 4:
                wait(sbuf.at[direction, distance - 1], bs_s.at[direction, distance - 1])
        wait(sbuf.at[direction, 3, direction], bs_s.at[direction, 3])
    for slot in range(8):
        wait(kv.at[:, chunk], sib_s.at[slot])
        wait(xsend.at[slot], bx_s.at[slot])
    for side in range(2):
        for slot in range(3):
            wait(relay.at[side], px_s.at[side, slot])
        wait(allq.at[xi], gx_s.at[side, 0])
        wait(relay.at[side], gx_s.at[side, 1])
    for i in range(1, XN):
        wait(dsum_own, dx_s.at[i])
    for i in range(1, ZN):
        wait(dz.at[0], dz_s.at[i])
        wait(zr.at[i], pz_s.at[i])
        wait(zr.at[i], gz_s.at[i])


def local(queries, keys, values, out_grad, depth_kernel, point_weight, block_of_frame):
    ctx, core = lax.axis_index("ctx"), lax.axis_index("tp") % 2
    chunk = 2 * (ctx // 2) + core
    blocks = block_of_frame.astype(jnp.int32)
    own = lax.dynamic_slice_in_dim(blocks, 2 * chunk, 2)
    own = jnp.repeat(own, FRAME)
    bound = jnp.where(blocks[:, None] <= own[None, :], OPEN, NEG).astype(F32)
    bound = bound.reshape(CN, 2, ROWS)
    kern = jnp.pad(depth_kernel.astype(F32), ((0, 5), (0, 0)))

    vmem = pl.BlockSpec(memory_space=pltpu.VMEM)
    dma = pltpu.SemaphoreType.DMA
    wide = (2, ROWS, COLS)
    scratch = [
        pltpu.VMEM((ROWS, COLS), BF16),
        pltpu.VMEM((2, CN, ROWS, COLS), BF16),
        pltpu.VMEM((TN, ROWS, COLS), BF16),
        pltpu.VMEM((32, COLS), F32),
        pltpu.VMEM((HEADS, 1, ROWS), F32),
        pltpu.VMEM((HEADS, 1, ROWS), F32),
        pltpu.VMEM((HEADS, HD, ROWS), F32),
        pltpu.VMEM((HEADS, 1, ROWS), F32),
        pltpu.VMEM((HEADS, 1, ROWS), F32),
        pltpu.VMEM((2, FRAME, COLS), BF16),
        pltpu.VMEM((4, FRAME, COLS), BF16),
        pltpu.VMEM((4, FRAME, COLS), BF16),
        pltpu.VMEM((3, 4, FRAME + 2 * WW, COLS), F32),
        pltpu.VMEM((ROWS, COLS), BF16),
        pltpu.VMEM((ROWS, COLS), BF16),
        pltpu.VMEM((32, COLS), F32),
        pltpu.VMEM((32, COLS), F32),
        pltpu.VMEM((ROWS, COLS), BF16),
        pltpu.VMEM((HEADS, HD, ROWS), F32),
        pltpu.VMEM(wide, F32),
        pltpu.VMEM((8,) + wide, BF16),
        pltpu.VMEM((8,) + wide, BF16),
        pltpu.VMEM((2, 4) + wide, BF16),
        pltpu.VMEM((2, 4) + wide, BF16),
        pltpu.VMEM((XN, 2, ZN, PIECE, COLS), BF16),
        pltpu.VMEM((2, 3, 2, ZN // 2, PIECE, COLS), BF16),
        pltpu.VMEM((2, 2, ZN // 2, PIECE, COLS), BF16),
        pltpu.VMEM((2, ZN, PIECE, COLS), BF16),
        pltpu.VMEM((ZN, 2, PIECE, COLS), BF16),
        pltpu.VMEM((XN, 2, ZN, PIECE, COLS), BF16),
        pltpu.VMEM((XN, 32, COLS), F32),
        pltpu.VMEM((ZN, 32, COLS), F32),
        pltpu.VMEM((3, ROWS, COLS), BF16),
        pltpu.VMEM((3, ROWS, COLS), BF16),
        dma((9,)), dma((9,)),
        dma((TN,)), dma((TN,)),
        dma((2, 4, 2)), dma((2, 4, 2)),
        dma((8,)), dma((8,)),
        dma((2, 2)), dma((2, 2)),
        dma((2, 4)), dma((2, 4)),
        dma((8,)), dma((8,)),
        dma((2, 3)), dma((2, 3)),
        dma((ZN,)), dma((ZN,)),
        dma((ZN,)), dma((ZN,)),
        dma((2, 2)), dma((2, 2)),
        dma((XN,)), dma((XN,)),
        dma((ZN,)), dma((ZN,)),
    ]
    rows = jax.ShapeDtypeStruct((ROWS, COLS), BF16)
    dq, dk, dv, point, depth = pl.pallas_call(
        body,
        out_shape=(
            rows, rows, rows,
            jax.ShapeDtypeStruct(point_weight.shape, F32),
            jax.ShapeDtypeStruct((32, COLS), F32),
        ),
        in_specs=[vmem] * 7,
        out_specs=(vmem,) * 5,
        scratch_shapes=scratch,
        compiler_params=pltpu.CompilerParams(
            collective_id=0, has_side_effects=True, vmem_limit_bytes=60 * 1024 * 1024
        ),
    )(queries[0], keys[0], values[0], out_grad[0], point_weight, kern, bound)
    return dq[None], dk[None], dv[None], point, depth[:27]


def solution(mesh):
    placed = (
        P("dp", "ctx", "tp"),
        P("dp", "ctx", "tp"),
        P("dp", "ctx", "tp"),
        P("dp", "ctx", "tp"),
        P(None, "tp"),
        P("tp", None),
        P(),
    )
    return jax.shard_map(
        local,
        mesh=mesh,
        in_specs=placed,
        out_specs=(
            P("dp", "ctx", "tp"),
            P("dp", "ctx", "tp"),
            P("dp", "ctx", "tp"),
            P("tp", None),
            P(None, "tp"),
        ),
        check_vma=False,
    )
```

time: 707 us -> 171 us (0.24)
  waiting for transfers between devices: 359 us -> 0 us
  Pallas kernels: 0 us -> 154 us
  blocking collectives: 113 us -> 0 us
  matrix products: 85.1 us -> 0 us
  local copies, waits for them, and re-layouts: 73.4 us -> 12.1 us
  other arithmetic: 39.6 us -> 2.07 us
  starting transfers between devices: 14.6 us -> 0 us
  between operations: 14.9 us -> 0.67 us
    all_gather x3 -> x0, waiting for transfers between devices: 195 us -> none  [the longest x1 90.1 us: local(): lax.all_gather(value_rows, 'ctx', axis=0, tiled=True)]
    reduce_scatter x1 -> x0, waiting for transfers between devices: 160 us -> none  [local(): lax.psum_scatter(key_terms.astype(jnp.bfloat16), 'ctx', scatter_dimension...]
    pallas_call x0 -> x1, Pallas kernels: none -> 154 us  [local(): pl.pallas_call(body, out_shape=(rows, rows, rows, jax.ShapeDtypeStruct(po...]
    psum x1 -> x0, blocking collectives: 113 us -> none  [local(): lax.psum((depth_local * grad_scale).astype(jnp.bfloat16), ('ctx', 'dp'))]
    dot_general x58 -> x0, matrix products: 85.1 us -> none  [the longest x16 32.7 us: masked_scores(): jnp.einsum('qhd,khd->hqk', query_heads, key_heads, preferred_element_type...]
    reduce_sum x14 -> x0, other arithmetic: 20.4 us -> none  [the longest x8 14 us: attend_step(): row_sum = row_sum * factor + jnp.sum(weights, axis=2)]
    dynamic_update_slice x16 -> x0, local copies, waits for them, and re-layouts: 18.9 us -> none  [key_step(): key_terms = lax.dynamic_update_slice_in_dim(key_terms, joined, first_row, 0)]
    ppermute x4 -> x0, starting transfers between devices: 14.2 us -> none  [the longest x2 11.6 us: with_halo(): lax.ppermute(tail, axis, [(i, (i + 1) % count) for i in range(ends)])]
  transfers between devices with their start and end apart: 9 -> 0, of which waited for: 6 -> 0; matrix products, arithmetic and copies ran while one was open for 16% -> 0% of each run, Pallas kernels for 0% -> 0%
where the time goes in v1:
time: 171 us; the launch traced here: 169 us
  Pallas kernels  154 us (90%)
  local copies, waits for them, and re-layouts  12.1 us (7%)
  other arithmetic  2.07 us (1%)
    pallas_call x1, Pallas kernels, local(): pl.pallas_call(body, out_shape=(rows, rows, rows, jax.ShapeDtypeStruct(po...  154 us
    unnamed x7, local copies, waits for them, and re-layouts  10.6 us

profile of v1, /device:TPU:1, one launch (start us, length us, event | category | flops | bytes accessed | tf_op | source)
XLA Modules:
  0.0 168.8 jit_solution(1301112052748901080)
XLA Ops:
  0.7 0.7 dynamic_slice.3
  1.4 0.1 broadcast_bitcast_fusion
  1.5 0.7 le.18
  2.2 0.7 compare_select_fusion.bound_ref
  2.9 1.4 pad_convert_fusion.kern_in
  4.3 154.0 %shard_map.110 = (bf16[256,384]{1,0:T(8,128)(2,1)}, bf16[256,384]{1,0:T(8,128)(2,1)}, bf16[256,384]{1,0:T(8,128)(2,1)}, f32[384,3072]{1,0:T(8,128)}, f32[32,384]{1,0:T(8,128)}) custom-call(bf16[256,384]{1,0:T(8,128)(2,1)} %bitcast.10, bf16[256,384]{1,0:T(8,128)(2,1)} %bitcast.11, bf16[256,384]{1,0:T(8,128)(2,1)} %bitcast.12, bf16[256,384]{1,0:T(8,128)(2,1)} %bitcast.13, ...), custom_call_target="tpu_custom_call" | custom-call | tf_op jit(solution)/shard_map/pallas_call | solution.py:645
  158.3 1.6 copy.17
  159.9 1.6 copy.18
  161.5 1.6 copy.19
  163.1 0.0 copy-start
  163.1 5.1 %copy.20 = f32[384,3072]{1,0:T(8,128)} copy(f32[384,3072]{1,0:T(8,128)} %get-tuple-element.23) | data formatting | bytes 9437184
  168.2 0.0 copy-done
  168.2 0.6 copy.21
Async XLA Ops:
  163.1 5.1 %copy-start = (f32[32,384]{1,0:T(8,128)S(1)}, f32[32,384]{1,0:T(8,128)}, u32[]{:S(2)}) copy-start(f32[32,384]{1,0:T(8,128)} %get-tuple-element.14) | copy-start | bytes 147460

commit v2 on v1

--- a/solution.py
+++ b/solution.py
@@ -43,28 +43,25 @@
     return lax.dot_general(a, b, (((0,), (0,)), ((), ())), preferred_element_type=F32)
 
 
-def spread_columns(shifted, plain):
+def spread_columns(shifted, plain, frame):
     column = lax.broadcasted_iota(jnp.int32, (FRAME, COLS), 0) % WW
-    for frame in range(4):
-        cells = plain[frame].astype(F32)
-        shifted[1, frame, WW : WW + FRAME] = cells
-        shifted[0, frame, WW : WW + FRAME] = jnp.where(
-            column > 0, pltpu.roll(cells, 1, 0), 0.0
-        )
-        shifted[2, frame, WW : WW + FRAME] = jnp.where(
-            column < WW - 1, pltpu.roll(cells, FRAME - 1, 0), 0.0
-        )
+    cells = plain[frame].astype(F32)
+    shifted[1, frame, WW : WW + FRAME] = cells
+    shifted[0, frame, WW : WW + FRAME] = jnp.where(column > 0, pltpu.roll(cells, 1, 0), 0.0)
+    shifted[2, frame, WW : WW + FRAME] = jnp.where(
+        column < WW - 1, pltpu.roll(cells, FRAME - 1, 0), 0.0
+    )
 
 
 def body(
-    q_in, k_in, v_in, g_in, w_ref, kern_in, bound_ref,
-    dq_out, dk_out, dv_out, point_out, depth_out,
-    q, kv, og, kern, row_max, row_sum, acc, lse, dots,
+    q_in, k_in, v_in, g_in, w_ref, kern_in, blocks,
+    rows_out, allq, depth_out,
+    q, kv, og, kern_send, kern, row_max, row_sum, acc, lse, dots,
     mg_send, mg_ext, at_ext, shifted, mixed, mixed_own, dsum, dsum_own,
     do, dq_acc, terms, xsend, xrecv, sbuf, rbuf,
-    prod, xr, relay, qsum, zr, allq, dx, dz, fin, finr,
+    prod, xr, relay, qsum, zs, zr, dx, dz, fin, finr,
     swap_s, swap_r, og_s, og_r, ring_s, ring_r, sib_s, sib_r, halo_s, halo_r,
-    bs_s, bs_r, bx_s, bx_r, px_s, px_r, pz_s, pz_r, gz_s, gz_r, gx_s, gx_r,
+    bs_s, bs_r, bx_s, bx_r, px_s, px_r, pz_s, pz_r, gz_s, gz_r, gx_s, gx_r, gy_s, gy_r,
     dx_s, dx_r, dz_s, dz_r,
 ):
     ctx, tp, dp = lax.axis_index("ctx"), lax.axis_index("tp"), lax.axis_index("dp")
@@ -123,7 +120,9 @@
     swap(0, k_in, kv.at[0, ctx])
     swap(1, v_in, kv.at[1, ctx])
     swap(2, q_in, q)
-    swap(3, kern_in, kern)
+    kern_send[...] = jnp.zeros_like(kern_send)
+    kern_send[0:27] = kern_in[...].astype(F32)
+    swap(3, kern_send, kern)
     for i in range(1, TN):
         send(g_in, og.at[tp], og_s.at[i], og_r.at[i], at_tp(i))
     keep = pltpu.make_async_copy(g_in, og.at[tp], og_r.at[0])
@@ -159,10 +158,19 @@
     def flip(index):
         return index + 1 - 2 * lax.rem(index, 2)
 
+    lane = lax.broadcasted_iota(jnp.int32, (1, ROWS), 1)
+    own_blocks = jnp.where(lane < FRAME, blocks[2 * chunk], blocks[2 * chunk + 1])
+
+    def limits_of(index):
+        return [
+            jnp.where(own_blocks >= blocks[2 * index + frame], OPEN, NEG).astype(F32)
+            for frame in range(2)
+        ]
+
     def fwd_chunk(index):
         @pl.when(index <= chunk + 2)
         def _():
-            limits = bound_ref[index]
+            limits = limits_of(index)
             for head in range(HEADS):
                 lanes = slice(head * HD, (head + 1) * HD)
                 keys = kv[0, index, :, lanes]
@@ -170,8 +178,8 @@
                 scores = nt(keys, q[:, lanes])
                 scores = jnp.concatenate(
                     [
-                        jnp.minimum(scores[:FRAME], limits[0:1]),
-                        jnp.minimum(scores[FRAME:], limits[1:2]),
+                        jnp.minimum(scores[:FRAME], limits[0]),
+                        jnp.minimum(scores[FRAME:], limits[1]),
                     ],
                     axis=0,
                 )
@@ -266,33 +274,10 @@
 
     fwd_step(3)
 
-    last = 2 * lax.rem(z + 4, ZN) + core
-    ring_wait(0, 4, 0, last)
-    ring_wait(1, 4, 1, last)
-    to_sibling(7, last)
-
-    def far(i, carry):
-        @pl.when(i == 1)
-        def _():
-            wait(kv.at[:, flip(last)], sib_r.at[7])
-
-        fwd_chunk(jnp.where(i == 0, last, flip(last)))
-        return carry
-
-    lax.fori_loop(0, 2, far, 0)
-
-    for head in range(HEADS):
-        lanes = slice(head * HD, (head + 1) * HD)
-        sums = row_sum[head]
-        lse[head] = row_max[head] * factor + jnp.log(sums) * math.log2(math.e)
-        rows = jnp.transpose(acc[head] / sums).astype(BF16)
-        at_ext[1, :, lanes] = rows[:FRAME]
-        at_ext[2, :, lanes] = rows[FRAME:]
-    halo(1, at_ext)
-
     wait(kern, swap_r.at[3])
     halo_wait(0, mg_ext)
-    spread_columns(shifted, mg_ext)
+    for frame in range(4):
+        spread_columns(shifted, mg_ext, frame)
 
     def taps():
         return [(a, r, c) for a in (-1, 0, 1) for r in (-1, 0, 1) for c in (-1, 0, 1)]
@@ -307,32 +292,38 @@
                 result = result + kern[tap : tap + 1, lanes] * window
             do[frame * FRAME : (frame + 1) * FRAME, lanes] = result.astype(BF16)
 
-    halo_wait(1, at_ext)
+    last = 2 * lax.rem(z + 4, ZN) + core
+    ring_wait(0, 4, 0, last)
+    ring_wait(1, 4, 1, last)
+    to_sibling(7, last)
+
+    def far(i, carry):
+        @pl.when(i == 1)
+        def _():
+            wait(kv.at[:, flip(last)], sib_r.at[7])
+
+        fwd_chunk(jnp.where(i == 0, last, flip(last)))
+        return carry
+
+    lax.fori_loop(0, 2, far, 0)
+
+    for head in range(HEADS):
+        lanes = slice(head * HD, (head + 1) * HD)
+        sums = row_sum[head]
+        lse[head] = row_max[head] * factor + jnp.log(sums) * math.log2(math.e)
+        rows = jnp.transpose(acc[head] / sums).astype(BF16)
+        at_ext[1, :, lanes] = rows[:FRAME]
+        at_ext[2, :, lanes] = rows[FRAME:]
+    halo(1, at_ext)
+
+    for frame in (1, 2):
+        spread_columns(shifted, at_ext, frame)
     for head in range(HEADS):
         lanes = slice(head * HD, (head + 1) * HD)
         attended = jnp.concatenate([at_ext[1, :, lanes], at_ext[2, :, lanes]], axis=0)
         product = attended.astype(F32) * do[:, lanes].astype(F32)
         dots[head] = jnp.sum(jnp.transpose(product), axis=0, keepdims=True)
 
-    spread_columns(shifted, at_ext)
-    dsum[...] = jnp.zeros_like(dsum)
-    grad_scale = 1.0 / math.sqrt(2.0 * CN * ROWS)
-    for frame in range(2):
-        for head in range(HEADS):
-            lanes = slice(head * HD, (head + 1) * HD)
-            result = jnp.zeros((FRAME, HD), F32)
-            grad = mg_ext[1 + frame, :, lanes].astype(F32)
-            for tap, (a, r, c) in enumerate(taps()):
-                first = WW + WW * r
-                window = shifted[1 + c, frame + 1 + a, first : first + FRAME, lanes]
-                result = result + kern[tap : tap + 1, lanes] * window
-                dsum[tap : tap + 1, lanes] += (
-                    jnp.sum(window * grad, axis=0, keepdims=True) * grad_scale
-                )
-            mixed[frame * FRAME : (frame + 1) * FRAME, lanes] = result.astype(BF16)
-    swap(5, mixed, mixed_own)
-    swap(6, dsum, dsum_own)
-
     def bwd_chunk(index):
         @pl.when(index > chunk + 2)
         def _():
@@ -340,7 +331,7 @@
 
         @pl.when(index <= chunk + 2)
         def _():
-            limits = bound_ref[index]
+            limits = limits_of(index)
             for head in range(HEADS):
                 lanes = slice(head * HD, (head + 1) * HD)
                 keys = kv[0, index, :, lanes]
@@ -350,8 +341,8 @@
                 scores = nt(keys, queries)
                 scores = jnp.concatenate(
                     [
-                        jnp.minimum(scores[:FRAME], limits[0:1]),
-                        jnp.minimum(scores[FRAME:], limits[1:2]),
+                        jnp.minimum(scores[:FRAME], limits[0]),
+                        jnp.minimum(scores[FRAME:], limits[1]),
                     ],
                     axis=0,
                 )
@@ -371,23 +362,20 @@
 
     target = 2 * lax.rem(z + 4, ZN) + core
 
-    def bwd_far(i, carry):
-        bwd_chunk(jnp.where(i == 0, flip(target), target))
-
-        @pl.when(i == 0)
-        def _():
-            share(7)
-
-        return carry
-
-    lax.fori_loop(0, 2, bwd_far, 0)
-    total = shared(7).astype(BF16)
-    sbuf[0, 3, 0] = total[0]
-    sbuf[1, 3, 1] = total[1]
-    send(sbuf.at[0, 3, 0], rbuf.at[0, 3, 0], bs_s.at[0, 3], bs_r.at[0, 3], at_z(1))
-    send(sbuf.at[1, 3, 1], rbuf.at[1, 3, 1], bs_s.at[1, 3], bs_r.at[1, 3], at_z(-1))
-
-    def bwd_step(distance):
+    def bwd_pair(slot, index, between):
+        def step(i, carry):
+            bwd_chunk(jnp.where(i == 0, flip(index), index))
+
+            @pl.when(i == 0)
+            def _():
+                share(slot)
+                between()
+
+            return carry
+
+        lax.fori_loop(0, 2, step, 0)
+
+    def bwd_step(distance, events):
         up = 2 * lax.rem(z + distance, ZN) + core
         down = 2 * lax.rem(z - distance + ZN, ZN) + core
 
@@ -416,137 +404,223 @@
                     (2 * goal + half, tp, dp),
                 )
 
+            for place, event in enumerate(events):
+                pl.when(i == place)(event)
             return carry
 
         lax.fori_loop(0, 4, step, 0)
 
-    wait(mixed_own, swap_r.at[5])
-
-    def product(i, carry):
-        block = tn(mixed_own[...], og[i]) * grad_scale
-        prod[i // 2, lax.rem(i, 2)] = block.astype(BF16).reshape(ZN, PIECE, COLS)
-        return carry
-
-    lax.fori_loop(0, TN, product, 0)
+    grad_scale = 1.0 / math.sqrt(2.0 * CN * ROWS)
     across = lax.rem(xi + 2, XN)
     right = lax.rem(xi + 1, XN)
     left = lax.rem(xi + 3, XN)
     lower, upper = slice(0, ZN // 2), slice(ZN // 2, ZN)
-    send(prod.at[across, :, lower], xr.at[0, 0], px_s.at[0, 0], px_r.at[0, 0], at_x(1))
-    send(prod.at[across, :, upper], xr.at[1, 0], px_s.at[1, 0], px_r.at[1, 0], at_x(-1))
-    send(prod.at[right, :, upper], xr.at[0, 1], px_s.at[0, 1], px_r.at[0, 1], at_x(1))
-    send(prod.at[left, :, lower], xr.at[1, 1], px_s.at[1, 1], px_r.at[1, 1], at_x(-1))
-    wait(dsum_own, swap_r.at[6])
-    for i in range(1, XN):
-        send(dsum_own, dx.at[i], dx_s.at[i], dx_r.at[i], at_x(i))
-
-    bwd_step(3)
-
-    wait(xr.at[0, 0], px_r.at[0, 0])
-    relay[0] = (prod[right, :, lower].astype(F32) + xr[0, 0].astype(F32)).astype(BF16)
-    send(relay.at[0], xr.at[0, 2], px_s.at[0, 2], px_r.at[0, 2], at_x(1))
-    wait(xr.at[1, 0], px_r.at[1, 0])
-    relay[1] = (prod[left, :, upper].astype(F32) + xr[1, 0].astype(F32)).astype(BF16)
-    send(relay.at[1], xr.at[1, 2], px_s.at[1, 2], px_r.at[1, 2], at_x(-1))
-    sums = dsum_own[...]
-    for i in range(1, XN):
-        wait(dx.at[i], dx_r.at[i])
-        sums = sums + dx[i]
-    dz[0] = sums
-    for i in range(1, ZN):
-        send(dz.at[0], dz.at[i], dz_s.at[i], dz_r.at[i], at_z(i))
-
-    bwd_step(2)
-
-    for side in range(2):
-        for slot in (1, 2):
-            wait(xr.at[side, slot], px_r.at[side, slot])
-    qsum[:, lower] = (
-        prod[xi, :, lower].astype(F32) + xr[0, 2].astype(F32) + xr[1, 1].astype(F32)
-    ).astype(BF16)
-    qsum[:, upper] = (
-        prod[xi, :, upper].astype(F32) + xr[0, 1].astype(F32) + xr[1, 2].astype(F32)
-    ).astype(BF16)
-    for i in range(1, ZN):
-        goal = lax.rem(z + i, ZN)
-        send(qsum.at[:, goal], zr.at[i], pz_s.at[i], pz_r.at[i], at_z(i))
-
-    bwd_step(1)
-
-    piece = qsum[:, z].astype(F32)
-    for i in range(1, ZN):
-        wait(zr.at[i], pz_r.at[i])
-        piece = piece + zr[i].astype(F32)
-    allq[xi, :, z] = piece.astype(BF16)
-    for i in range(1, ZN):
-        send(allq.at[xi, :, z], allq.at[xi, :, z], gz_s.at[i], gz_r.at[i], at_z(i))
-
-    def bwd_own(i, carry):
-        bwd_chunk(jnp.where(i == 0, flip(chunk), chunk))
-
-        @pl.when(i == 0)
-        def _():
-            share(0)
-
-        return carry
-
-    lax.fori_loop(0, 2, bwd_own, 0)
+
+    def mix():
+        halo_wait(1, at_ext)
+        for frame in (0, 3):
+            spread_columns(shifted, at_ext, frame)
+        dsum[...] = jnp.zeros_like(dsum)
+        for frame in range(2):
+            for head in range(HEADS):
+                lanes = slice(head * HD, (head + 1) * HD)
+                result = jnp.zeros((FRAME, HD), F32)
+                grad = mg_ext[1 + frame, :, lanes].astype(F32)
+                for tap, (a, r, c) in enumerate(taps()):
+                    first = WW + WW * r
+                    window = shifted[1 + c, frame + 1 + a, first : first + FRAME, lanes]
+                    result = result + kern[tap : tap + 1, lanes] * window
+                    dsum[tap : tap + 1, lanes] += (
+                        jnp.sum(window * grad, axis=0, keepdims=True) * grad_scale
+                    )
+                mixed[frame * FRAME : (frame + 1) * FRAME, lanes] = result.astype(BF16)
+        swap(5, mixed, mixed_own)
+        swap(6, dsum, dsum_own)
+
+    def raw_sends(b):
+        send(prod.at[across, b, lower], xr.at[b, 0, 0], px_s.at[b, 0, 0], px_r.at[b, 0, 0], at_x(1))
+        send(prod.at[across, b, upper], xr.at[b, 1, 0], px_s.at[b, 1, 0], px_r.at[b, 1, 0], at_x(-1))
+        send(prod.at[right, b, upper], xr.at[b, 0, 1], px_s.at[b, 0, 1], px_r.at[b, 0, 1], at_x(1))
+        send(prod.at[left, b, lower], xr.at[b, 1, 1], px_s.at[b, 1, 1], px_r.at[b, 1, 1], at_x(-1))
+
+    def products():
+        wait(mixed_own, swap_r.at[5])
+        for b in range(2):
+
+            def product(quarter, carry, b=b):
+                block = tn(mixed_own[...], og[2 * quarter + b]) * grad_scale
+                prod[quarter, b] = block.astype(BF16).reshape(ZN, PIECE, COLS)
+                return carry
+
+            lax.fori_loop(0, XN, product, 0)
+            if b == 0:
+                raw_sends(0)
+        wait(dsum_own, swap_r.at[6])
+        for i in range(1, XN):
+            send(dsum_own, dx.at[i], dx_s.at[i], dx_r.at[i], at_x(i))
+
+    def relays(b):
+        wait(xr.at[b, 0, 0], px_r.at[b, 0, 0])
+        relay[b, 0] = (prod[right, b, lower].astype(F32) + xr[b, 0, 0].astype(F32)).astype(BF16)
+        send(relay.at[b, 0], xr.at[b, 0, 2], px_s.at[b, 0, 2], px_r.at[b, 0, 2], at_x(1))
+        wait(xr.at[b, 1, 0], px_r.at[b, 1, 0])
+        relay[b, 1] = (prod[left, b, upper].astype(F32) + xr[b, 1, 0].astype(F32)).astype(BF16)
+        send(relay.at[b, 1], xr.at[b, 1, 2], px_s.at[b, 1, 2], px_r.at[b, 1, 2], at_x(-1))
+
+    def z_place(side, distance):
+        return lax.rem(z + ZN + (distance if side == 0 else -distance), ZN)
+
+    def z_send(b, side, distance, sums):
+        zs[b, side, distance - 1] = sums.astype(BF16)
+        send(
+            zs.at[b, side, distance - 1], zr.at[b, side, distance - 1],
+            pz_s.at[b, side, distance - 1], pz_r.at[b, side, distance - 1],
+            at_z(1 if side == 0 else -1),
+        )
+
+    def z_first(b):
+        for side in range(2):
+            for slot in (1, 2):
+                wait(xr.at[b, side, slot], px_r.at[b, side, slot])
+        qsum[b, lower] = (
+            prod[xi, b, lower].astype(F32) + xr[b, 0, 2].astype(F32) + xr[b, 1, 1].astype(F32)
+        )
+        qsum[b, upper] = (
+            prod[xi, b, upper].astype(F32) + xr[b, 0, 1].astype(F32) + xr[b, 1, 2].astype(F32)
+        )
+        z_send(b, b, 4, qsum[b, z_place(b, 4)])
+
+    def z_arrived(b, side, distance):
+        wait(zr.at[b, side, distance - 1], pz_r.at[b, side, distance - 1])
+        return zr[b, side, distance - 1].astype(F32)
+
+    def z_next(b, distance):
+        for side in (b, 1 - b):
+            sums = qsum[b, z_place(side, distance)]
+            if distance < 3 or side == b:
+                sums = sums + z_arrived(b, side, distance + 1)
+            z_send(b, side, distance, sums)
+
+    def pass_z(b, side, distance, place):
+        piece = allq.at[xi, b, place]
+        send(
+            piece, piece, gz_s.at[b, side, distance - 1], gz_r.at[b, side, distance - 1],
+            at_z(1 if side == 0 else -1),
+        )
+
+    def pass_x(b, slot, place):
+        piece = allq.at[xi, b, place]
+        for side in range(2):
+            send(
+                piece, piece, gx_s.at[b, side, slot], gx_r.at[b, side, slot],
+                at_x(1 if side == 0 else -1),
+            )
+
+    def z_last(b):
+        allq[xi, b, z] = (
+            qsum[b, z] + z_arrived(b, 0, 1) + z_arrived(b, 1, 1)
+        ).astype(BF16)
+        for side in range(2):
+            pass_z(b, side, 1, z)
+        pass_x(b, 0, z)
+
+    def z_gather(b, distance):
+        for side in range(2):
+            if distance == 4 and side != b:
+                continue
+            place = z_place(side, -distance)
+            wait(allq.at[xi, b, place], gz_r.at[b, side, distance - 1])
+            if distance < 3 or (distance == 3 and side == b):
+                pass_z(b, side, distance + 1, place)
+            pass_x(b, 7 if distance == 4 else distance + 3 * side, place)
+
+    def x_relay(b):
+        for slot in range(ZN):
+            wait(allq.at[left, b, 0], gx_r.at[b, 0, slot])
+        here = allq.at[left, b, lower]
+        send(here, here, gy_s.at[b, 0], gy_r.at[b, 0], at_x(1))
+        for slot in range(ZN):
+            wait(allq.at[right, b, 0], gx_r.at[b, 1, slot])
+        here = allq.at[right, b, upper]
+        send(here, here, gy_s.at[b, 1], gy_r.at[b, 1], at_x(-1))
+
+    def depth_z():
+        sums = dsum_own[...]
+        for i in range(1, XN):
+            wait(dx.at[i], dx_r.at[i])
+            sums = sums + dx[i]
+        dz[0] = sums
+        for i in range(1, ZN):
+            send(dz.at[0], dz.at[i], dz_s.at[i], dz_r.at[i], at_z(i))
+
+    def both(*events):
+        def run():
+            for event in events:
+                event()
+
+        return run
+
+    def ev(f, *values):
+        return lambda: f(*values)
+
+    bwd_pair(7, target, mix)
+    total = shared(7).astype(BF16)
+    sbuf[0, 3, 0] = total[0]
+    sbuf[1, 3, 1] = total[1]
+    send(sbuf.at[0, 3, 0], rbuf.at[0, 3, 0], bs_s.at[0, 3], bs_r.at[0, 3], at_z(1))
+    send(sbuf.at[1, 3, 1], rbuf.at[1, 3, 1], bs_s.at[1, 3], bs_r.at[1, 3], at_z(-1))
+    products()
+    bwd_step(3, [
+        lambda: None, both(ev(relays, 0), ev(raw_sends, 1)), depth_z, lambda: None,
+    ])
+    bwd_step(2, [
+        ev(z_first, 0),
+        both(ev(relays, 1), ev(z_next, 0, 3)),
+        ev(z_next, 0, 2),
+        both(ev(z_next, 0, 1), ev(z_first, 1)),
+    ])
+    bwd_step(1, [
+        both(ev(z_last, 0), ev(z_next, 1, 3)),
+        both(ev(z_gather, 0, 1), ev(z_next, 1, 2)),
+        both(ev(z_gather, 0, 2), ev(z_next, 1, 1)),
+        both(ev(z_gather, 0, 3), ev(z_last, 1)),
+    ])
+    bwd_pair(0, chunk, both(ev(z_gather, 0, 4), ev(z_gather, 1, 1)))
     for head in range(HEADS):
         lanes = slice(head * HD, (head + 1) * HD)
         fin[0, :, lanes] = (jnp.transpose(dq_acc[head]) * scaling).astype(BF16)
     swap(7, fin.at[0], finr.at[0])
+    z_gather(1, 2)
+    z_gather(1, 3)
+    z_gather(1, 4)
     total = shared(0)
     for side in range(2):
         wait(rbuf.at[side, 0], bs_r.at[side, 0])
         total = total + rbuf[side, 0].astype(F32)
     fin[1:3] = total.astype(BF16)
     swap(8, fin.at[1:3], finr.at[1:3])
-
-    for i in range(1, ZN):
-        goal = lax.rem(z + ZN - i, ZN)
-        wait(allq.at[xi, :, goal], gz_r.at[i])
-    send(allq.at[xi], allq.at[xi], gx_s.at[0, 0], gx_r.at[0, 0], at_x(1))
-    send(allq.at[xi], allq.at[xi], gx_s.at[1, 0], gx_r.at[1, 0], at_x(-1))
+    x_relay(0)
+    x_relay(1)
 
     sums = dz[0]
     for i in range(1, ZN):
         wait(dz.at[i], dz_r.at[i])
         sums = sums + dz[i]
     depth_out[...] = sums
-
-    def put(quarter):
-        for block in range(2):
-            cells = allq[quarter, block].reshape(COLS, COLS).astype(F32)
-            first = pl.multiple_of((2 * quarter + block) * COLS, HD)
-            point_out[:, pl.ds(first, COLS)] = cells
-
-    put(xi)
-    wait(allq.at[left], gx_r.at[0, 0])
-    send(
-        allq.at[left, :, lower], allq.at[left, :, lower], gx_s.at[0, 1], gx_r.at[0, 1], at_x(1)
-    )
-    wait(allq.at[right], gx_r.at[1, 0])
-    send(
-        allq.at[right, :, upper], allq.at[right, :, upper], gx_s.at[1, 1], gx_r.at[1, 1],
-        at_x(-1),
-    )
-    put(left)
-    put(right)
     wait(finr.at[0], swap_r.at[7])
-    dq_out[...] = finr[0]
+    rows_out[0] = finr[0]
     wait(finr.at[1:3], swap_r.at[8])
-    dk_out[...] = finr[1]
-    dv_out[...] = finr[2]
-    wait(allq.at[across, :, lower], gx_r.at[0, 1])
-    wait(allq.at[across, :, upper], gx_r.at[1, 1])
-    put(across)
+    rows_out[1:3] = finr[1:3]
+    for b in range(2):
+        wait(allq.at[across, b, lower], gy_r.at[b, 0])
+        wait(allq.at[across, b, upper], gy_r.at[b, 1])
 
     @pl.when(off)
     def _():
         wait(k_in, swap_s.at[0])
         wait(v_in, swap_s.at[1])
         wait(q_in, swap_s.at[2])
-        wait(kern_in, swap_s.at[3])
+        wait(kern_send, swap_s.at[3])
         wait(mg_send, swap_s.at[4])
         wait(mixed, swap_s.at[5])
         wait(dsum, swap_s.at[6])
@@ -566,29 +640,34 @@
     for slot in range(8):
         wait(kv.at[:, chunk], sib_s.at[slot])
         wait(xsend.at[slot], bx_s.at[slot])
-    for side in range(2):
-        for slot in range(3):
-            wait(relay.at[side], px_s.at[side, slot])
-        wait(allq.at[xi], gx_s.at[side, 0])
-        wait(relay.at[side], gx_s.at[side, 1])
     for i in range(1, XN):
         wait(dsum_own, dx_s.at[i])
     for i in range(1, ZN):
         wait(dz.at[0], dz_s.at[i])
-        wait(zr.at[i], pz_s.at[i])
-        wait(zr.at[i], gz_s.at[i])
+    for b in range(2):
+        for side in range(2):
+            for slot in range(3):
+                wait(relay.at[b, side], px_s.at[b, side, slot])
+            for distance in range(1, 5):
+                if distance < 4 or side == b:
+                    wait(zs.at[b, side, distance - 1], pz_s.at[b, side, distance - 1])
+                    wait(zs.at[b, side, distance - 1], gz_s.at[b, side, distance - 1])
+            for slot in range(ZN):
+                wait(zs.at[b, side, 0], gx_s.at[b, side, slot])
+            wait(relay.at[b, side], gy_s.at[b, side])
+
+
+def finish(rows_ref, quarters, depth_ref, dq_out, dk_out, dv_out, point_out, depth_out):
+    dq_out[0] = rows_ref[0]
+    dk_out[0] = rows_ref[1]
+    dv_out[0] = rows_ref[2]
+    for block in range(TN):
+        cells = quarters[block // 2, block % 2].reshape(COLS, COLS).astype(F32)
+        point_out[:, block * COLS : (block + 1) * COLS] = cells
+    depth_out[...] = depth_ref[0:27]
 
 
 def local(queries, keys, values, out_grad, depth_kernel, point_weight, block_of_frame):
-    ctx, core = lax.axis_index("ctx"), lax.axis_index("tp") % 2
-    chunk = 2 * (ctx // 2) + core
-    blocks = block_of_frame.astype(jnp.int32)
-    own = lax.dynamic_slice_in_dim(blocks, 2 * chunk, 2)
-    own = jnp.repeat(own, FRAME)
-    bound = jnp.where(blocks[:, None] <= own[None, :], OPEN, NEG).astype(F32)
-    bound = bound.reshape(CN, 2, ROWS)
-    kern = jnp.pad(depth_kernel.astype(F32), ((0, 5), (0, 0)))
-
     vmem = pl.BlockSpec(memory_space=pltpu.VMEM)
     dma = pltpu.SemaphoreType.DMA
     wide = (2, ROWS, COLS)
@@ -596,6 +675,7 @@
         pltpu.VMEM((ROWS, COLS), BF16),
         pltpu.VMEM((2, CN, ROWS, COLS), BF16),
         pltpu.VMEM((TN, ROWS, COLS), BF16),
+        pltpu.VMEM((32, COLS), F32),
         pltpu.VMEM((32, COLS), F32),
         pltpu.VMEM((HEADS, 1, ROWS), F32),
         pltpu.VMEM((HEADS, 1, ROWS), F32),
@@ -618,11 +698,11 @@
         pltpu.VMEM((2, 4) + wide, BF16),
         pltpu.VMEM((2, 4) + wide, BF16),
         pltpu.VMEM((XN, 2, ZN, PIECE, COLS), BF16),
-        pltpu.VMEM((2, 3, 2, ZN // 2, PIECE, COLS), BF16),
+        pltpu.VMEM((2, 2, 3, ZN // 2, PIECE, COLS), BF16),
         pltpu.VMEM((2, 2, ZN // 2, PIECE, COLS), BF16),
-        pltpu.VMEM((2, ZN, PIECE, COLS), BF16),
-        pltpu.VMEM((ZN, 2, PIECE, COLS), BF16),
-        pltpu.VMEM((XN, 2, ZN, PIECE, COLS), BF16),
+        pltpu.VMEM((2, ZN, PIECE, COLS), F32),
+        pltpu.VMEM((2, 2, 4, PIECE, COLS), BF16),
+        pltpu.VMEM((2, 2, 4, PIECE, COLS), BF16),
         pltpu.VMEM((XN, 32, COLS), F32),
         pltpu.VMEM((ZN, 32, COLS), F32),
         pltpu.VMEM((3, ROWS, COLS), BF16),
@@ -634,29 +714,42 @@
         dma((2, 2)), dma((2, 2)),
         dma((2, 4)), dma((2, 4)),
         dma((8,)), dma((8,)),
-        dma((2, 3)), dma((2, 3)),
-        dma((ZN,)), dma((ZN,)),
-        dma((ZN,)), dma((ZN,)),
+        dma((2, 2, 3)), dma((2, 2, 3)),
+        dma((2, 2, 4)), dma((2, 2, 4)),
+        dma((2, 2, 4)), dma((2, 2, 4)),
+        dma((2, 2, ZN)), dma((2, 2, ZN)),
         dma((2, 2)), dma((2, 2)),
         dma((XN,)), dma((XN,)),
         dma((ZN,)), dma((ZN,)),
     ]
-    rows = jax.ShapeDtypeStruct((ROWS, COLS), BF16)
-    dq, dk, dv, point, depth = pl.pallas_call(
+    rows, quarters, depth = pl.pallas_call(
         body,
         out_shape=(
-            rows, rows, rows,
-            jax.ShapeDtypeStruct(point_weight.shape, F32),
+            jax.ShapeDtypeStruct((3, ROWS, COLS), BF16),
+            jax.ShapeDtypeStruct((XN, 2, ZN, PIECE, COLS), BF16),
             jax.ShapeDtypeStruct((32, COLS), F32),
         ),
-        in_specs=[vmem] * 7,
-        out_specs=(vmem,) * 5,
+        in_specs=[vmem] * 6 + [pl.BlockSpec(memory_space=pltpu.SMEM)],
+        out_specs=(vmem,) * 3,
         scratch_shapes=scratch,
         compiler_params=pltpu.CompilerParams(
             collective_id=0, has_side_effects=True, vmem_limit_bytes=60 * 1024 * 1024
         ),
-    )(queries[0], keys[0], values[0], out_grad[0], point_weight, kern, bound)
-    return dq[None], dk[None], dv[None], point, depth[:27]
+        name="layer_backward",
+    )(queries[0], keys[0], values[0], out_grad[0], point_weight, depth_kernel, block_of_frame)
+    part = jax.ShapeDtypeStruct((1, ROWS, COLS), BF16)
+    return pl.pallas_call(
+        finish,
+        out_shape=(
+            part, part, part,
+            jax.ShapeDtypeStruct(point_weight.shape, F32),
+            jax.ShapeDtypeStruct(depth_kernel.shape, F32),
+        ),
+        in_specs=[vmem] * 3,
+        out_specs=(vmem,) * 5,
+        compiler_params=pltpu.CompilerParams(vmem_limit_bytes=32 * 1024 * 1024),
+        name="write_outputs",
+    )(rows, quarters, depth)
 
 
 def solution(mesh):

time: 171 us -> 154 us (0.901)
  local copies, waits for them, and re-layouts: 12.1 us -> 3.52 us
  Pallas kernels: 154 us -> 149 us
  other arithmetic: 2.07 us -> 0 us
    unnamed x7 -> x6, local copies, waits for them, and re-layouts: 10.6 us -> 3.52 us
    pallas_call x1 -> x2, Pallas kernels: 154 us -> 149 us  [the longest x1 147 us: local(): pl.pallas_call(body, out_shape=(jax.ShapeDtypeStruct((3, ROWS, COLS), BF1...]
where the time goes in v2:
time: 154 us; the launch traced here: 153 us
  Pallas kernels  149 us (97%)
  local copies, waits for them, and re-layouts  3.52 us (2%)
    pallas_call x1, Pallas kernels, local(): pl.pallas_call(body, out_shape=(jax.ShapeDtypeStruct((3, ROWS, COLS), BF1...  147 us
    unnamed x6, local copies, waits for them, and re-layouts  3.52 us

profile of v2, /device:TPU:1, one launch (start us, length us, event | category | flops | bytes accessed | tf_op | source)
XLA Modules:
  0.0 153.4 jit_solution(10757017861009427742)
XLA Ops:
  0.6 146.6 %layer_backward.1 = (bf16[3,256,384]{2,1,0:T(8,128)(2,1)}, bf16[4,2,8,48,384]{4,3,2,1,0:T(8,128)(2,1)}, f32[32,384]{1,0:T(8,128)}) custom-call(bf16[256,384]{1,0:T(8,128)(2,1)} %bitcast.4, bf16[256,384]{1,0:T(8,128)(2,1)} %bitcast.5, bf16[256,384]{1,0:T(8,128)(2,1)} %bitcast.6, bf16[256,384]{1,0:T(8,128)(2,1)} %bitcast.7, bf16[384,3072]{1,0:T(8,128)(2,1)} %w_ref.1, ...), custom_call_target="tpu_custom_call" | custom-call | tf_op jit(solution)/shard_map/layer_backward/pallas_call | solution.py:725
  147.2 0.0 copy-start
  147.2 1.7 %copy-done = bf16[4,2,8,48,384]{4,3,2,1,0:T(8,128)(2,1)S(1)} copy-done((bf16[4,2,8,48,384]{4,3,2,1,0:T(8,128)(2,1)S(1)}, bf16[4,2,8,48,384]{4,3,2,1,0:T(8,128)(2,1)}, u32[]{:S(2)}) %copy-start) | copy-done | bytes 2359320
  148.9 0.0 copy-start.1
  148.9 1.1 copy-done.1
  150.0 0.0 copy-start.2
  150.0 0.8 copy-done.2
  150.8 2.7 %write_outputs.1 = (bf16[1,256,384]{2,1,0:T(8,128)(2,1)}, bf16[1,256,384]{2,1,0:T(8,128)(2,1)}, bf16[1,256,384]{2,1,0:T(8,128)(2,1)}, f32[384,3072]{1,0:T(8,128)}, f32[27,384]{1,0:T(8,128)}) custom-call(bf16[3,256,384]{2,1,0:T(8,128)(2,1)S(1)} %copy-done.1, bf16[4,2,8,48,384]{4,3,2,1,0:T(8,128)(2,1)S(1)} %copy-done, f32[32,384]{1,0:T(8,128)S(1)} %copy-done.2), custom_call_target="tpu_custom_call" | custom-call | tf_op jit(solution)/shard_map/write_outputs/pallas_call | solution.py:741
Async XLA Ops:
  147.2 1.7 %copy-start = (bf16[4,2,8,48,384]{4,3,2,1,0:T(8,128)(2,1)S(1)}, bf16[4,2,8,48,384]{4,3,2,1,0:T(8,128)(2,1)}, u32[]{:S(2)}) copy-start(bf16[4,2,8,48,384]{4,3,2,1,0:T(8,128)(2,1)} %get-tuple-element.9.quarters) | copy-start | bytes 7077892
  148.9 1.1 copy-start.1
  150.0 0.8 copy-start.2

commit v3 on v2

--- a/solution.py
+++ b/solution.py
@@ -54,15 +54,15 @@
 
 
 def body(
-    q_in, k_in, v_in, g_in, w_ref, kern_in, blocks,
-    rows_out, allq, depth_out,
+    q_in, k_in, v_in, g_in, w_in, kern_in, blocks,
+    rows_out, quarters_out, depth_out,
     q, kv, og, kern_send, kern, row_max, row_sum, acc, lse, dots,
-    mg_send, mg_ext, at_ext, shifted, mixed, mixed_own, dsum, dsum_own,
+    w_ref, mg_send, mg_ext, at_ext, shifted, mixed, mixed_all, dsum, dsum_send, ogx,
     do, dq_acc, terms, xsend, xrecv, sbuf, rbuf,
-    prod, xr, relay, qsum, zs, zr, dx, dz, fin, finr,
+    qsum, zs, zr, allq, dx, dz, depth, fin, finr, out_sem,
     swap_s, swap_r, og_s, og_r, ring_s, ring_r, sib_s, sib_r, halo_s, halo_r,
-    bs_s, bs_r, bx_s, bx_r, px_s, px_r, pz_s, pz_r, gz_s, gz_r, gx_s, gx_r, gy_s, gy_r,
-    dx_s, dx_r, dz_s, dz_r,
+    bs_s, bs_r, bx_s, bx_r, ox_s, ox_r, oy_s, oy_r, pz_s, pz_r, gz_s, gz_r,
+    gx_s, gx_r, gy_s, gy_r, mb_s, mb_r, dx_s, dx_r, dz_s, dz_r,
 ):
     ctx, tp, dp = lax.axis_index("ctx"), lax.axis_index("tp"), lax.axis_index("dp")
     z, half = ctx // 2, ctx % 2
@@ -81,6 +81,14 @@
         place = lax.rem(xi + step + XN, XN)
         return (2 * z + place // 2, tp, lax.rem(place, 2))
 
+    def crossed(step):
+        place = lax.rem(xi + step + XN, XN)
+        return (2 * z + place // 2, 2 * y + 1 - core, lax.rem(place, 2))
+
+    def at_half(step):
+        place = lax.rem(xi + step + XN, XN)
+        return (2 * z + place // 2, 2 * y + half, lax.rem(place, 2))
+
     def at_tp(step):
         return (ctx, lax.rem(tp + step, TN), dp)
 
@@ -97,7 +105,8 @@
     peers = [at_tp(i) for i in range(1, TN)]
     peers += [at_z(i) for i in range(1, ZN)]
     peers += [at_x(i) for i in range(1, XN)]
-    peers += [partner, halo_dev]
+    peers += [crossed(i) for i in range(1, XN)]
+    peers += [halo_dev]
     for device in peers:
         pl.semaphore_signal(barrier, inc=1, device_id=device, device_id_type=MESH)
     pl.semaphore_wait(barrier, len(peers))
@@ -127,6 +136,8 @@
         send(g_in, og.at[tp], og_s.at[i], og_r.at[i], at_tp(i))
     keep = pltpu.make_async_copy(g_in, og.at[tp], og_r.at[0])
     keep.start()
+    weights_in = pltpu.make_async_copy(w_in, w_ref, out_sem.at[0])
+    weights_in.start()
 
     acc[...] = jnp.zeros_like(acc)
     row_sum[...] = jnp.zeros_like(row_sum)
@@ -135,6 +146,9 @@
     shifted[...] = jnp.zeros_like(shifted)
     rbuf[0, 3, 1] = jnp.zeros((ROWS, COLS), BF16)
     rbuf[1, 3, 0] = jnp.zeros((ROWS, COLS), BF16)
+    zr[0, 3, 1] = jnp.zeros((PIECE, COLS), BF16)
+    zr[1, 3, 0] = jnp.zeros((PIECE, COLS), BF16)
+    dsum[...] = jnp.zeros_like(dsum)
 
     def ring(direction, distance, part, source):
         place = kv.at[part, source]
@@ -233,12 +247,20 @@
     keep.wait()
     for i in range(1, TN):
         wait(og.at[lax.rem(tp + TN - i, TN)], og_r.at[i])
+    weights_in.wait()
     total = nt(og[0], w_ref[:, 0:COLS])
     for i in range(1, TN):
         total += nt(og[i], w_ref[:, i * COLS : (i + 1) * COLS])
     mg_send[...] = total.astype(BF16).reshape(2, FRAME, COLS)
     swap(4, mg_send, mg_ext.at[1:3])
 
+    quarter = og.at[pl.ds(2 * xi, 2)]
+    own_quarter = pltpu.make_async_copy(quarter, ogx.at[xi], ox_r.at[0])
+    own_quarter.start()
+    for i in range(1, XN):
+        goal = lax.rem(xi + i, XN)
+        send(og.at[2 * goal + core], ogx.at[xi, core], ox_s.at[i], ox_r.at[i], at_x(i))
+
     fwd_step(2)
 
     def halo(which, ext):
@@ -271,6 +293,10 @@
 
     wait(mg_ext.at[1:3], swap_r.at[4])
     halo(0, mg_ext)
+    for i in range(1, XN):
+        place = ogx.at[lax.rem(xi + XN - i, XN), core]
+        wait(place, ox_r.at[i])
+        send(place, place, oy_s.at[i], oy_r.at[i], sibling)
 
     fwd_step(3)
 
@@ -392,15 +418,16 @@
             @pl.when(i >= 2)
             def _():
                 if distance == 3:
-                    wait(rbuf.at[side, 3, side], bs_r.at[side, 3])
+                    wait(rbuf.at[side, 3, side], bs_r.at[side, 3, side])
                 else:
-                    wait(rbuf.at[side, distance], bs_r.at[side, distance])
+                    for part in range(2):
+                        wait(rbuf.at[side, distance, part], bs_r.at[side, distance, part])
                 added = shared(slot) + rbuf[side, distance].astype(F32)
                 sbuf[side, distance - 1] = added.astype(BF16)
                 goal = lax.rem(z + ZN + 1 - 2 * side, ZN)
                 send(
-                    sbuf.at[side, distance - 1], rbuf.at[side, distance - 1],
-                    bs_s.at[side, distance - 1], bs_r.at[side, distance - 1],
+                    sbuf.at[side, distance - 1, 0], rbuf.at[side, distance - 1, 0],
+                    bs_s.at[side, distance - 1, 0], bs_r.at[side, distance - 1, 0],
                     (2 * goal + half, tp, dp),
                 )
 
@@ -420,138 +447,155 @@
         halo_wait(1, at_ext)
         for frame in (0, 3):
             spread_columns(shifted, at_ext, frame)
-        dsum[...] = jnp.zeros_like(dsum)
         for frame in range(2):
             for head in range(HEADS):
                 lanes = slice(head * HD, (head + 1) * HD)
                 result = jnp.zeros((FRAME, HD), F32)
-                grad = mg_ext[1 + frame, :, lanes].astype(F32)
                 for tap, (a, r, c) in enumerate(taps()):
                     first = WW + WW * r
                     window = shifted[1 + c, frame + 1 + a, first : first + FRAME, lanes]
                     result = result + kern[tap : tap + 1, lanes] * window
-                    dsum[tap : tap + 1, lanes] += (
-                        jnp.sum(window * grad, axis=0, keepdims=True) * grad_scale
-                    )
                 mixed[frame * FRAME : (frame + 1) * FRAME, lanes] = result.astype(BF16)
-        swap(5, mixed, mixed_own)
-        swap(6, dsum, dsum_own)
-
-    def raw_sends(b):
-        send(prod.at[across, b, lower], xr.at[b, 0, 0], px_s.at[b, 0, 0], px_r.at[b, 0, 0], at_x(1))
-        send(prod.at[across, b, upper], xr.at[b, 1, 0], px_s.at[b, 1, 0], px_r.at[b, 1, 0], at_x(-1))
-        send(prod.at[right, b, upper], xr.at[b, 0, 1], px_s.at[b, 0, 1], px_r.at[b, 0, 1], at_x(1))
-        send(prod.at[left, b, lower], xr.at[b, 1, 1], px_s.at[b, 1, 1], px_r.at[b, 1, 1], at_x(-1))
+        spread_out(mixed, mixed_all, mb_s, mb_r)
+
+    def spread_out(src, dst, send_sems, recv_sems):
+        slot = 2 * core + dp
+        for i in range(1, XN):
+            send(src, dst.at[slot], send_sems.at[i], recv_sems.at[slot], at_half(i))
+
+        @pl.when(off)
+        def _():
+            send(src, dst.at[slot], send_sems.at[0], recv_sems.at[slot], sibling)
+
+        @pl.when(same)
+        def _():
+            pltpu.make_async_copy(src, dst.at[slot], recv_sems.at[slot]).start()
+
+    def tap_sums():
+        for head in range(HEADS):
+            lanes = slice(head * HD, (head + 1) * HD)
+            for tap, (a, r, c) in enumerate(taps()):
+                first = WW + WW * r
+                sums = jnp.zeros((1, HD), F32)
+                for frame in range(2):
+                    window = shifted[1 + c, frame + 1 + a, first : first + FRAME, lanes]
+                    grad = mg_ext[1 + frame, :, lanes].astype(F32)
+                    sums = sums + jnp.sum(window * grad, axis=0, keepdims=True)
+                dsum[tap : tap + 1, lanes] = sums * grad_scale
+        dsum_send[...] = dsum[...].astype(BF16)
+        spread_out(dsum_send, dx, dx_s, dx_r)
 
     def products():
-        wait(mixed_own, swap_r.at[5])
-        for b in range(2):
-
-            def product(quarter, carry, b=b):
-                block = tn(mixed_own[...], og[2 * quarter + b]) * grad_scale
-                prod[quarter, b] = block.astype(BF16).reshape(ZN, PIECE, COLS)
-                return carry
-
-            lax.fori_loop(0, XN, product, 0)
-            if b == 0:
-                raw_sends(0)
-        wait(dsum_own, swap_r.at[6])
+        own_quarter.wait()
         for i in range(1, XN):
-            send(dsum_own, dx.at[i], dx_s.at[i], dx_r.at[i], at_x(i))
-
-    def relays(b):
-        wait(xr.at[b, 0, 0], px_r.at[b, 0, 0])
-        relay[b, 0] = (prod[right, b, lower].astype(F32) + xr[b, 0, 0].astype(F32)).astype(BF16)
-        send(relay.at[b, 0], xr.at[b, 0, 2], px_s.at[b, 0, 2], px_r.at[b, 0, 2], at_x(1))
-        wait(xr.at[b, 1, 0], px_r.at[b, 1, 0])
-        relay[b, 1] = (prod[left, b, upper].astype(F32) + xr[b, 1, 0].astype(F32)).astype(BF16)
-        send(relay.at[b, 1], xr.at[b, 1, 2], px_s.at[b, 1, 2], px_r.at[b, 1, 2], at_x(-1))
+            wait(ogx.at[lax.rem(xi + XN - i, XN), 1 - core], oy_r.at[i])
+        for slot in range(XN):
+            wait(mixed_all.at[slot], mb_r.at[slot])
+            for b in range(2):
+                block = (tn(mixed_all[slot], ogx[slot, b]) * grad_scale).reshape(ZN, PIECE, COLS)
+                qsum[:, b] = block if slot == 0 else qsum[:, b] + block
 
     def z_place(side, distance):
         return lax.rem(z + ZN + (distance if side == 0 else -distance), ZN)
 
-    def z_send(b, side, distance, sums):
-        zs[b, side, distance - 1] = sums.astype(BF16)
+    def z_send(side, distance, sums):
+        zs[side, distance - 1] = sums.astype(BF16)
         send(
-            zs.at[b, side, distance - 1], zr.at[b, side, distance - 1],
-            pz_s.at[b, side, distance - 1], pz_r.at[b, side, distance - 1],
+            zs.at[side, distance - 1], zr.at[side, distance - 1],
+            pz_s.at[side, distance - 1], pz_r.at[side, distance - 1],
             at_z(1 if side == 0 else -1),
         )
 
-    def z_first(b):
+    def z_first():
+        sums = qsum[z_place(0, 4)].astype(BF16)
         for side in range(2):
-            for slot in (1, 2):
-                wait(xr.at[b, side, slot], px_r.at[b, side, slot])
-        qsum[b, lower] = (
-            prod[xi, b, lower].astype(F32) + xr[b, 0, 2].astype(F32) + xr[b, 1, 1].astype(F32)
-        )
-        qsum[b, upper] = (
-            prod[xi, b, upper].astype(F32) + xr[b, 0, 1].astype(F32) + xr[b, 1, 2].astype(F32)
-        )
-        z_send(b, b, 4, qsum[b, z_place(b, 4)])
-
-    def z_arrived(b, side, distance):
-        wait(zr.at[b, side, distance - 1], pz_r.at[b, side, distance - 1])
-        return zr[b, side, distance - 1].astype(F32)
-
-    def z_next(b, distance):
-        for side in (b, 1 - b):
-            sums = qsum[b, z_place(side, distance)]
-            if distance < 3 or side == b:
-                sums = sums + z_arrived(b, side, distance + 1)
-            z_send(b, side, distance, sums)
-
-    def pass_z(b, side, distance, place):
-        piece = allq.at[xi, b, place]
+            zs[side, 3, side] = sums[side]
+            send(
+                zs.at[side, 3, side], zr.at[side, 3, side],
+                pz_s.at[side, 3], pz_r.at[side, 3], at_z(1 if side == 0 else -1),
+            )
+
+    def z_arrived(side, distance):
+        if distance == 4:
+            wait(zr.at[side, 3, side], pz_r.at[side, 3])
+        else:
+            wait(zr.at[side, distance - 1], pz_r.at[side, distance - 1])
+        return zr[side, distance - 1].astype(F32)
+
+    def z_next(distance):
+        for side in range(2):
+            sums = qsum[z_place(side, distance)] + z_arrived(side, distance + 1)
+            z_send(side, distance, sums)
+
+    def pass_z(side, distance, piece):
         send(
-            piece, piece, gz_s.at[b, side, distance - 1], gz_r.at[b, side, distance - 1],
+            piece, piece, gz_s.at[side, distance - 1], gz_r.at[side, distance - 1],
             at_z(1 if side == 0 else -1),
         )
 
-    def pass_x(b, slot, place):
-        piece = allq.at[xi, b, place]
+    def pass_x(slot, place):
+        piece = allq.at[xi, place]
         for side in range(2):
             send(
-                piece, piece, gx_s.at[b, side, slot], gx_r.at[b, side, slot],
+                piece, piece, gx_s.at[side, slot], gx_r.at[side, slot],
                 at_x(1 if side == 0 else -1),
             )
 
-    def z_last(b):
-        allq[xi, b, z] = (
-            qsum[b, z] + z_arrived(b, 0, 1) + z_arrived(b, 1, 1)
-        ).astype(BF16)
+    def z_last():
+        allq[xi, z] = (qsum[z] + z_arrived(0, 1) + z_arrived(1, 1)).astype(BF16)
         for side in range(2):
-            pass_z(b, side, 1, z)
-        pass_x(b, 0, z)
-
-    def z_gather(b, distance):
+            pass_z(side, 1, allq.at[xi, z])
+        pass_x(0, z)
+
+    def z_gather(distance):
         for side in range(2):
-            if distance == 4 and side != b:
-                continue
             place = z_place(side, -distance)
-            wait(allq.at[xi, b, place], gz_r.at[b, side, distance - 1])
-            if distance < 3 or (distance == 3 and side == b):
-                pass_z(b, side, distance + 1, place)
-            pass_x(b, 7 if distance == 4 else distance + 3 * side, place)
-
-    def x_relay(b):
+            wait(allq.at[xi, place], gz_r.at[side, distance - 1])
+            if distance < 3:
+                pass_z(side, distance + 1, allq.at[xi, place])
+            else:
+                pass_z(side, 4, allq.at[xi, place, side])
+            pass_x(distance + 3 * side, place)
+
+    def z_gather_far():
+        place = z_place(0, 4)
+        for side in range(2):
+            wait(allq.at[xi, place, side], gz_r.at[side, 3])
+        pass_x(7, place)
+
+    def put(quarter, i):
+        pltpu.make_async_copy(allq.at[quarter], quarters_out.at[quarter], out_sem.at[i]).start()
+
+    def x_relay():
+        put(xi, 1)
         for slot in range(ZN):
-            wait(allq.at[left, b, 0], gx_r.at[b, 0, slot])
-        here = allq.at[left, b, lower]
-        send(here, here, gy_s.at[b, 0], gy_r.at[b, 0], at_x(1))
+            wait(allq.at[left, 0], gx_r.at[0, slot])
+        here = allq.at[left, lower]
+        send(here, here, gy_s.at[0], gy_r.at[0], at_x(1))
         for slot in range(ZN):
-            wait(allq.at[right, b, 0], gx_r.at[b, 1, slot])
-        here = allq.at[right, b, upper]
-        send(here, here, gy_s.at[b, 1], gy_r.at[b, 1], at_x(-1))
+            wait(allq.at[right, 0], gx_r.at[1, slot])
+        here = allq.at[right, upper]
+        send(here, here, gy_s.at[1], gy_r.at[1], at_x(-1))
+        put(left, 2)
+        put(right, 3)
 
     def depth_z():
-        sums = dsum_own[...]
-        for i in range(1, XN):
-            wait(dx.at[i], dx_r.at[i])
-            sums = sums + dx[i]
-        dz[0] = sums
+        for slot in range(XN):
+            wait(dx.at[slot], dx_r.at[slot])
+        sums = dx[0].astype(F32) + dx[1].astype(F32) + dx[2].astype(F32) + dx[3].astype(F32)
+        dz[0] = sums.astype(BF16)
         for i in range(1, ZN):
             send(dz.at[0], dz.at[i], dz_s.at[i], dz_r.at[i], at_z(i))
+
+    def terms_send(side, distance, part):
+        def run():
+            send(
+                sbuf.at[side, distance - 1, part], rbuf.at[side, distance - 1, part],
+                bs_s.at[side, distance - 1, part], bs_r.at[side, distance - 1, part],
+                at_z(1 if side == 0 else -1),
+            )
+
+        return run
 
     def both(*events):
         def run():
@@ -563,57 +607,61 @@
     def ev(f, *values):
         return lambda: f(*values)
 
+    def nothing():
+        pass
+
     bwd_pair(7, target, mix)
     total = shared(7).astype(BF16)
     sbuf[0, 3, 0] = total[0]
     sbuf[1, 3, 1] = total[1]
-    send(sbuf.at[0, 3, 0], rbuf.at[0, 3, 0], bs_s.at[0, 3], bs_r.at[0, 3], at_z(1))
-    send(sbuf.at[1, 3, 1], rbuf.at[1, 3, 1], bs_s.at[1, 3], bs_r.at[1, 3], at_z(-1))
+    terms_send(0, 4, 0)()
+    terms_send(1, 4, 1)()
+    bwd_step(3, [tap_sums, nothing, nothing, terms_send(0, 3, 1)])
     products()
-    bwd_step(3, [
-        lambda: None, both(ev(relays, 0), ev(raw_sends, 1)), depth_z, lambda: None,
-    ])
+    z_first()
+    terms_send(1, 3, 1)()
     bwd_step(2, [
-        ev(z_first, 0),
-        both(ev(relays, 1), ev(z_next, 0, 3)),
-        ev(z_next, 0, 2),
-        both(ev(z_next, 0, 1), ev(z_first, 1)),
+        ev(z_next, 3),
+        both(ev(z_next, 2), depth_z),
+        ev(z_next, 1),
+        both(z_last, terms_send(0, 2, 1)),
     ])
     bwd_step(1, [
-        both(ev(z_last, 0), ev(z_next, 1, 3)),
-        both(ev(z_gather, 0, 1), ev(z_next, 1, 2)),
-        both(ev(z_gather, 0, 2), ev(z_next, 1, 1)),
-        both(ev(z_gather, 0, 3), ev(z_last, 1)),
+        both(ev(z_gather, 1), terms_send(1, 2, 1)),
+        nothing,
+        ev(z_gather, 2),
+        terms_send(0, 1, 1),
     ])
-    bwd_pair(0, chunk, both(ev(z_gather, 0, 4), ev(z_gather, 1, 1)))
+    terms_send(1, 1, 1)()
+    bwd_pair(0, chunk, ev(z_gather, 3))
     for head in range(HEADS):
         lanes = slice(head * HD, (head + 1) * HD)
         fin[0, :, lanes] = (jnp.transpose(dq_acc[head]) * scaling).astype(BF16)
     swap(7, fin.at[0], finr.at[0])
-    z_gather(1, 2)
-    z_gather(1, 3)
-    z_gather(1, 4)
+    z_gather_far()
     total = shared(0)
     for side in range(2):
-        wait(rbuf.at[side, 0], bs_r.at[side, 0])
+        for part in range(2):
+            wait(rbuf.at[side, 0, part], bs_r.at[side, 0, part])
         total = total + rbuf[side, 0].astype(F32)
     fin[1:3] = total.astype(BF16)
     swap(8, fin.at[1:3], finr.at[1:3])
-    x_relay(0)
-    x_relay(1)
-
-    sums = dz[0]
+    x_relay()
+
+    sums = dz[0].astype(F32)
     for i in range(1, ZN):
         wait(dz.at[i], dz_r.at[i])
-        sums = sums + dz[i]
-    depth_out[...] = sums
+        sums = sums + dz[i].astype(F32)
+    depth[...] = sums[0:27]
+    depth_copy = pltpu.make_async_copy(depth, depth_out, out_sem.at[5])
+    depth_copy.start()
     wait(finr.at[0], swap_r.at[7])
-    rows_out[0] = finr[0]
     wait(finr.at[1:3], swap_r.at[8])
-    rows_out[1:3] = finr[1:3]
-    for b in range(2):
-        wait(allq.at[across, b, lower], gy_r.at[b, 0])
-        wait(allq.at[across, b, upper], gy_r.at[b, 1])
+    rows_copy = pltpu.make_async_copy(finr, rows_out, out_sem.at[6])
+    rows_copy.start()
+    wait(allq.at[across, lower], gy_r.at[0])
+    wait(allq.at[across, upper], gy_r.at[1])
+    put(across, 4)
 
     @pl.when(off)
     def _():
@@ -622,8 +670,8 @@
         wait(q_in, swap_s.at[2])
         wait(kern_send, swap_s.at[3])
         wait(mg_send, swap_s.at[4])
-        wait(mixed, swap_s.at[5])
-        wait(dsum, swap_s.at[6])
+        wait(mixed, mb_s.at[0])
+        wait(dsum_send, dx_s.at[0])
         wait(fin.at[0], swap_s.at[7])
         wait(fin.at[1:3], swap_s.at[8])
 
@@ -634,41 +682,67 @@
             for part in range(2):
                 if distance < 4 or part == direction:
                     wait(kv.at[part, chunk], ring_s.at[direction, distance - 1, part])
-            if distance < 4:
-                wait(sbuf.at[direction, distance - 1], bs_s.at[direction, distance - 1])
-        wait(sbuf.at[direction, 3, direction], bs_s.at[direction, 3])
+                    wait(sbuf.at[direction, 0, part], bs_s.at[direction, distance - 1, part])
     for slot in range(8):
         wait(kv.at[:, chunk], sib_s.at[slot])
         wait(xsend.at[slot], bx_s.at[slot])
     for i in range(1, XN):
-        wait(dsum_own, dx_s.at[i])
+        wait(mixed, mb_s.at[i])
+        wait(dsum_send, dx_s.at[i])
+        wait(mixed, ox_s.at[i])
+        wait(mixed, oy_s.at[i])
     for i in range(1, ZN):
         wait(dz.at[0], dz_s.at[i])
-    for b in range(2):
-        for side in range(2):
-            for slot in range(3):
-                wait(relay.at[b, side], px_s.at[b, side, slot])
-            for distance in range(1, 5):
-                if distance < 4 or side == b:
-                    wait(zs.at[b, side, distance - 1], pz_s.at[b, side, distance - 1])
-                    wait(zs.at[b, side, distance - 1], gz_s.at[b, side, distance - 1])
-            for slot in range(ZN):
-                wait(zs.at[b, side, 0], gx_s.at[b, side, slot])
-            wait(relay.at[b, side], gy_s.at[b, side])
-
-
-def finish(rows_ref, quarters, depth_ref, dq_out, dk_out, dv_out, point_out, depth_out):
-    dq_out[0] = rows_ref[0]
-    dk_out[0] = rows_ref[1]
-    dv_out[0] = rows_ref[2]
-    for block in range(TN):
-        cells = quarters[block // 2, block % 2].reshape(COLS, COLS).astype(F32)
-        point_out[:, block * COLS : (block + 1) * COLS] = cells
-    depth_out[...] = depth_ref[0:27]
+    for side in range(2):
+        for distance in range(1, 4):
+            wait(zs.at[side, 0], pz_s.at[side, distance - 1])
+            wait(zs.at[side, 0], gz_s.at[side, distance - 1])
+        wait(zs.at[side, 3, side], pz_s.at[side, 3])
+        wait(zs.at[side, 3, side], gz_s.at[side, 3])
+        for slot in range(ZN):
+            wait(zs.at[side, 0], gx_s.at[side, slot])
+        wait(allq.at[xi, lower], gy_s.at[side])
+    for i in range(1, 5):
+        wait(allq.at[xi], out_sem.at[i])
+    depth_copy.wait()
+    rows_copy.wait()
+
+
+def finish(
+    rows_in, quarters, depth_in, dq_out, dk_out, dv_out, point_out, depth_out,
+    blocks, cells, load, store, small,
+):
+    loads = [
+        pltpu.make_async_copy(quarters.at[i // 2, :, i % 2], blocks.at[i], load.at[i])
+        for i in range(TN)
+    ]
+    for copy in loads:
+        copy.start()
+    others = [
+        pltpu.make_async_copy(rows_in.at[0], dq_out.at[0], small.at[0]),
+        pltpu.make_async_copy(rows_in.at[1], dk_out.at[0], small.at[1]),
+        pltpu.make_async_copy(rows_in.at[2], dv_out.at[0], small.at[2]),
+        pltpu.make_async_copy(depth_in, depth_out, small.at[3]),
+    ]
+    for copy in others:
+        copy.start()
+    stores = []
+    for i in range(TN):
+        loads[i].wait()
+        cells[i] = blocks[i].reshape(COLS, COLS).astype(F32)
+        stores.append(
+            pltpu.make_async_copy(
+                cells.at[i], point_out.at[:, i * COLS : (i + 1) * COLS], store.at[i]
+            )
+        )
+        stores[i].start()
+    for copy in stores + others:
+        copy.wait()
 
 
 def local(queries, keys, values, out_grad, depth_kernel, point_weight, block_of_frame):
     vmem = pl.BlockSpec(memory_space=pltpu.VMEM)
+    hbm = pl.BlockSpec(memory_space=pl.ANY)
     dma = pltpu.SemaphoreType.DMA
     wide = (2, ROWS, COLS)
     scratch = [
@@ -682,14 +756,16 @@
         pltpu.VMEM((HEADS, HD, ROWS), F32),
         pltpu.VMEM((HEADS, 1, ROWS), F32),
         pltpu.VMEM((HEADS, 1, ROWS), F32),
+        pltpu.VMEM(point_weight.shape, BF16),
         pltpu.VMEM((2, FRAME, COLS), BF16),
         pltpu.VMEM((4, FRAME, COLS), BF16),
         pltpu.VMEM((4, FRAME, COLS), BF16),
         pltpu.VMEM((3, 4, FRAME + 2 * WW, COLS), F32),
         pltpu.VMEM((ROWS, COLS), BF16),
-        pltpu.VMEM((ROWS, COLS), BF16),
+        pltpu.VMEM((XN, ROWS, COLS), BF16),
         pltpu.VMEM((32, COLS), F32),
-        pltpu.VMEM((32, COLS), F32),
+        pltpu.VMEM((32, COLS), BF16),
+        pltpu.VMEM((XN, 2, ROWS, COLS), BF16),
         pltpu.VMEM((ROWS, COLS), BF16),
         pltpu.VMEM((HEADS, HD, ROWS), F32),
         pltpu.VMEM(wide, F32),
@@ -697,28 +773,30 @@
         pltpu.VMEM((8,) + wide, BF16),
         pltpu.VMEM((2, 4) + wide, BF16),
         pltpu.VMEM((2, 4) + wide, BF16),
-        pltpu.VMEM((XN, 2, ZN, PIECE, COLS), BF16),
-        pltpu.VMEM((2, 2, 3, ZN // 2, PIECE, COLS), BF16),
-        pltpu.VMEM((2, 2, ZN // 2, PIECE, COLS), BF16),
-        pltpu.VMEM((2, ZN, PIECE, COLS), F32),
-        pltpu.VMEM((2, 2, 4, PIECE, COLS), BF16),
-        pltpu.VMEM((2, 2, 4, PIECE, COLS), BF16),
-        pltpu.VMEM((XN, 32, COLS), F32),
-        pltpu.VMEM((ZN, 32, COLS), F32),
+        pltpu.VMEM((ZN, 2, PIECE, COLS), F32),
+        pltpu.VMEM((2, 4, 2, PIECE, COLS), BF16),
+        pltpu.VMEM((2, 4, 2, PIECE, COLS), BF16),
+        pltpu.VMEM((XN, ZN, 2, PIECE, COLS), BF16),
+        pltpu.VMEM((XN, 32, COLS), BF16),
+        pltpu.VMEM((ZN, 32, COLS), BF16),
+        pltpu.VMEM((27, COLS), F32),
         pltpu.VMEM((3, ROWS, COLS), BF16),
         pltpu.VMEM((3, ROWS, COLS), BF16),
+        dma((7,)),
         dma((9,)), dma((9,)),
         dma((TN,)), dma((TN,)),
         dma((2, 4, 2)), dma((2, 4, 2)),
         dma((8,)), dma((8,)),
         dma((2, 2)), dma((2, 2)),
+        dma((2, 4, 2)), dma((2, 4, 2)),
+        dma((8,)), dma((8,)),
+        dma((XN,)), dma((XN,)),
+        dma((XN,)), dma((XN,)),
         dma((2, 4)), dma((2, 4)),
-        dma((8,)), dma((8,)),
-        dma((2, 2, 3)), dma((2, 2, 3)),
-        dma((2, 2, 4)), dma((2, 2, 4)),
-        dma((2, 2, 4)), dma((2, 2, 4)),
-        dma((2, 2, ZN)), dma((2, 2, ZN)),
-        dma((2, 2)), dma((2, 2)),
+        dma((2, 4)), dma((2, 4)),
+        dma((2, ZN)), dma((2, ZN)),
+        dma((2,)), dma((2,)),
+        dma((XN,)), dma((XN,)),
         dma((XN,)), dma((XN,)),
         dma((ZN,)), dma((ZN,)),
     ]
@@ -726,11 +804,11 @@
         body,
         out_shape=(
             jax.ShapeDtypeStruct((3, ROWS, COLS), BF16),
-            jax.ShapeDtypeStruct((XN, 2, ZN, PIECE, COLS), BF16),
-            jax.ShapeDtypeStruct((32, COLS), F32),
+            jax.ShapeDtypeStruct((XN, ZN, 2, PIECE, COLS), BF16),
+            jax.ShapeDtypeStruct(depth_kernel.shape, F32),
         ),
-        in_specs=[vmem] * 6 + [pl.BlockSpec(memory_space=pltpu.SMEM)],
-        out_specs=(vmem,) * 3,
+        in_specs=[hbm] * 5 + [vmem, pl.BlockSpec(memory_space=pltpu.SMEM)],
+        out_specs=(hbm,) * 3,
         scratch_shapes=scratch,
         compiler_params=pltpu.CompilerParams(
             collective_id=0, has_side_effects=True, vmem_limit_bytes=60 * 1024 * 1024
@@ -745,8 +823,13 @@
             jax.ShapeDtypeStruct(point_weight.shape, F32),
             jax.ShapeDtypeStruct(depth_kernel.shape, F32),
         ),
-        in_specs=[vmem] * 3,
-        out_specs=(vmem,) * 5,
+        in_specs=[hbm] * 3,
+        out_specs=(hbm,) * 5,
+        scratch_shapes=[
+            pltpu.VMEM((TN, ZN, PIECE, COLS), BF16),
+            pltpu.VMEM((TN, COLS, COLS), F32),
+            dma((TN,)), dma((TN,)), dma((4,)),
+        ],
         compiler_params=pltpu.CompilerParams(vmem_limit_bytes=32 * 1024 * 1024),
         name="write_outputs",
     )(rows, quarters, depth)

time: 154 us -> 134 us (0.87)
  Pallas kernels: 149 us -> 128 us
    pallas_call x1, Pallas kernels: 147 us -> 125 us  [local(): pl.pallas_call(body, out_shape=(jax.ShapeDtypeStruct((3, ROWS, COLS), BF1...]
where the time goes in v3:
time: 134 us; the launch traced here: 133 us
  Pallas kernels  128 us (96%)
  local copies, waits for them, and re-layouts  3.52 us (3%)
    pallas_call x1, Pallas kernels, local(): pl.pallas_call(body, out_shape=(jax.ShapeDtypeStruct((3, ROWS, COLS), BF1...  125 us
    unnamed x6, local copies, waits for them, and re-layouts  3.52 us
    pallas_call x1, Pallas kernels, local(): pl.pallas_call(finish, out_shape=(part, part, part, jax.ShapeDtypeStruct(...  2.74 us

profile of v3, /device:TPU:1, one launch (start us, length us, event | category | flops | bytes accessed | tf_op | source)
XLA Modules:
  0.0 132.5 jit_solution(17051856488607230775)
XLA Ops:
  0.6 125.4 %layer_backward.1 = (bf16[3,256,384]{2,1,0:T(8,128)(2,1)}, bf16[4,8,2,48,384]{4,3,2,1,0:T(8,128)(2,1)}, f32[27,384]{1,0:T(8,128)}) custom-call(bf16[256,384]{1,0:T(8,128)(2,1)} %bitcast.4, bf16[256,384]{1,0:T(8,128)(2,1)} %bitcast.5, bf16[256,384]{1,0:T(8,128)(2,1)} %bitcast.6, bf16[256,384]{1,0:T(8,128)(2,1)} %bitcast.7, bf16[384,3072]{1,0:T(8,128)(2,1)} %w_in.1, ...), custom_call_target="tpu_custom_call" | custom-call | tf_op jit(solution)/shard_map/layer_backward/pallas_call | solution.py:803
  126.1 0.0 copy-start
  126.1 1.7 %copy-done = bf16[4,8,2,48,384]{4,3,2,1,0:T(8,128)(2,1)S(1)} copy-done((bf16[4,8,2,48,384]{4,3,2,1,0:T(8,128)(2,1)S(1)}, bf16[4,8,2,48,384]{4,3,2,1,0:T(8,128)(2,1)}, u32[]{:S(2)}) %copy-start) | copy-done | bytes 2359320
  127.8 0.0 copy-start.1
  127.8 1.1 copy-done.1
  128.8 0.0 copy-start.2
  128.8 0.8 copy-done.2
  129.6 2.7 %write_outputs.1 = (bf16[1,256,384]{2,1,0:T(8,128)(2,1)}, bf16[1,256,384]{2,1,0:T(8,128)(2,1)}, bf16[1,256,384]{2,1,0:T(8,128)(2,1)}, f32[384,3072]{1,0:T(8,128)}, f32[27,384]{1,0:T(8,128)}) custom-call(bf16[3,256,384]{2,1,0:T(8,128)(2,1)S(1)} %copy-done.1, bf16[4,8,2,48,384]{4,3,2,1,0:T(8,128)(2,1)S(1)} %copy-done, f32[27,384]{1,0:T(8,128)S(1)} %copy-done.2), custom_call_target="tpu_custom_call" | custom-call | tf_op jit(solution)/shard_map/write_outputs/pallas_call | solution.py:819
Async XLA Ops:
  126.1 1.7 %copy-start = (bf16[4,8,2,48,384]{4,3,2,1,0:T(8,128)(2,1)S(1)}, bf16[4,8,2,48,384]{4,3,2,1,0:T(8,128)(2,1)}, u32[]{:S(2)}) copy-start(bf16[4,8,2,48,384]{4,3,2,1,0:T(8,128)(2,1)} %get-tuple-element.9.quarters) | copy-start | bytes 7077892
  127.8 1.1 copy-start.1
  128.8 0.8 copy-start.2

commit v4 on v3

--- a/solution.py
+++ b/solution.py
@@ -388,6 +388,29 @@
 
     target = 2 * lax.rem(z + 4, ZN) + core
 
+    def terms_to(side, distance, part, device):
+        rows = pl.ds((part % 2) * FRAME, FRAME)
+        send(
+            sbuf.at[side, distance - 1, part // 2, rows],
+            rbuf.at[side, distance - 1, part // 2, rows],
+            bs_s.at[side, distance - 1, part], bs_r.at[side, distance - 1, part], device,
+        )
+
+    def terms_wait(side, distance, part):
+        rows = pl.ds((part % 2) * FRAME, FRAME)
+        wait(rbuf.at[side, distance - 1, part // 2, rows], bs_r.at[side, distance - 1, part])
+
+    def terms_wait_far(side, part):
+        rows = pl.ds(part * FRAME, FRAME)
+        wait(rbuf.at[side, 3, side, rows], bs_r.at[side, 3, 2 * side + part])
+
+    def terms_send(distance, part):
+        def run():
+            for side in range(2):
+                terms_to(side, distance, part, at_z(1 if side == 0 else -1))
+
+        return run
+
     def bwd_pair(slot, index, between):
         def step(i, carry):
             bwd_chunk(jnp.where(i == 0, flip(index), index))
@@ -418,18 +441,15 @@
             @pl.when(i >= 2)
             def _():
                 if distance == 3:
-                    wait(rbuf.at[side, 3, side], bs_r.at[side, 3, side])
+                    for part in range(2):
+                        terms_wait_far(side, part)
                 else:
-                    for part in range(2):
-                        wait(rbuf.at[side, distance, part], bs_r.at[side, distance, part])
+                    for part in range(4):
+                        terms_wait(side, distance + 1, part)
                 added = shared(slot) + rbuf[side, distance].astype(F32)
                 sbuf[side, distance - 1] = added.astype(BF16)
                 goal = lax.rem(z + ZN + 1 - 2 * side, ZN)
-                send(
-                    sbuf.at[side, distance - 1, 0], rbuf.at[side, distance - 1, 0],
-                    bs_s.at[side, distance - 1, 0], bs_r.at[side, distance - 1, 0],
-                    (2 * goal + half, tp, dp),
-                )
+                terms_to(side, distance, 0, (2 * goal + half, tp, dp))
 
             for place, event in enumerate(events):
                 pl.when(i == place)(event)
@@ -441,7 +461,6 @@
     across = lax.rem(xi + 2, XN)
     right = lax.rem(xi + 1, XN)
     left = lax.rem(xi + 3, XN)
-    lower, upper = slice(0, ZN // 2), slice(ZN // 2, ZN)
 
     def mix():
         halo_wait(1, at_ext)
@@ -556,6 +575,11 @@
             else:
                 pass_z(side, 4, allq.at[xi, place, side])
             pass_x(distance + 3 * side, place)
+        if distance == 1:
+            x_relay(0)
+        else:
+            x_relay(distance - 1)
+            x_relay(distance + 2)
 
     def z_gather_far():
         place = z_place(0, 4)
@@ -566,18 +590,19 @@
     def put(quarter, i):
         pltpu.make_async_copy(allq.at[quarter], quarters_out.at[quarter], out_sem.at[i]).start()
 
-    def x_relay():
-        put(xi, 1)
-        for slot in range(ZN):
-            wait(allq.at[left, 0], gx_r.at[0, slot])
-        here = allq.at[left, lower]
-        send(here, here, gy_s.at[0], gy_r.at[0], at_x(1))
-        for slot in range(ZN):
-            wait(allq.at[right, 0], gx_r.at[1, slot])
-        here = allq.at[right, upper]
-        send(here, here, gy_s.at[1], gy_r.at[1], at_x(-1))
-        put(left, 2)
-        put(right, 3)
+    def slot_place(slot):
+        if slot == 7:
+            return z_place(0, 4)
+        return z_place(0, -slot) if slot <= 3 else z_place(0, slot - 3)
+
+    def x_relay(slot):
+        place = slot_place(slot)
+        wait(allq.at[left, place], gx_r.at[0, slot])
+        here = allq.at[left, place, 0]
+        send(here, here, gy_s.at[0, slot], gy_r.at[0, slot], at_x(1))
+        wait(allq.at[right, place], gx_r.at[1, slot])
+        here = allq.at[right, place, 1]
+        send(here, here, gy_s.at[1, slot], gy_r.at[1, slot], at_x(-1))
 
     def depth_z():
         for slot in range(XN):
@@ -587,16 +612,6 @@
         for i in range(1, ZN):
             send(dz.at[0], dz.at[i], dz_s.at[i], dz_r.at[i], at_z(i))
 
-    def terms_send(side, distance, part):
-        def run():
-            send(
-                sbuf.at[side, distance - 1, part], rbuf.at[side, distance - 1, part],
-                bs_s.at[side, distance - 1, part], bs_r.at[side, distance - 1, part],
-                at_z(1 if side == 0 else -1),
-            )
-
-        return run
-
     def both(*events):
         def run():
             for event in events:
@@ -614,39 +629,43 @@
     total = shared(7).astype(BF16)
     sbuf[0, 3, 0] = total[0]
     sbuf[1, 3, 1] = total[1]
-    terms_send(0, 4, 0)()
-    terms_send(1, 4, 1)()
-    bwd_step(3, [tap_sums, nothing, nothing, terms_send(0, 3, 1)])
+    for part in range(2):
+        terms_to(0, 4, part, at_z(1))
+        terms_to(1, 4, 2 + part, at_z(-1))
+    bwd_step(3, [tap_sums, nothing, nothing, both(*[terms_send(3, part) for part in (1, 2, 3)])])
     products()
     z_first()
-    terms_send(1, 3, 1)()
     bwd_step(2, [
+        nothing,
         ev(z_next, 3),
-        both(ev(z_next, 2), depth_z),
-        ev(z_next, 1),
-        both(z_last, terms_send(0, 2, 1)),
+        nothing,
+        both(ev(z_next, 2), terms_send(2, 1)),
     ])
     bwd_step(1, [
-        both(ev(z_gather, 1), terms_send(1, 2, 1)),
-        nothing,
-        ev(z_gather, 2),
-        terms_send(0, 1, 1),
+        both(ev(z_next, 1), terms_send(2, 2)),
+        both(z_last, terms_send(2, 3)),
+        ev(z_gather, 1),
+        both(ev(z_gather, 2), terms_send(1, 1)),
     ])
-    terms_send(1, 1, 1)()
-    bwd_pair(0, chunk, ev(z_gather, 3))
+    bwd_pair(0, chunk, both(ev(z_gather, 3), terms_send(1, 2), terms_send(1, 3), depth_z))
     for head in range(HEADS):
         lanes = slice(head * HD, (head + 1) * HD)
         fin[0, :, lanes] = (jnp.transpose(dq_acc[head]) * scaling).astype(BF16)
     swap(7, fin.at[0], finr.at[0])
     z_gather_far()
+    put(xi, 1)
     total = shared(0)
-    for side in range(2):
-        for part in range(2):
-            wait(rbuf.at[side, 0, part], bs_r.at[side, 0, part])
-        total = total + rbuf[side, 0].astype(F32)
-    fin[1:3] = total.astype(BF16)
-    swap(8, fin.at[1:3], finr.at[1:3])
-    x_relay()
+    for part in range(2):
+        for side in range(2):
+            terms_wait(side, 1, 2 * part)
+            terms_wait(side, 1, 2 * part + 1)
+        done = total[part] + rbuf[0, 0, part].astype(F32) + rbuf[1, 0, part].astype(F32)
+        fin[1 + part] = done.astype(BF16)
+        swap(8 if part == 0 else 5, fin.at[1 + part], finr.at[1 + part])
+        if part == 0:
+            x_relay(3)
+            x_relay(6)
+    x_relay(7)
 
     sums = dz[0].astype(F32)
     for i in range(1, ZN):
@@ -656,11 +675,15 @@
     depth_copy = pltpu.make_async_copy(depth, depth_out, out_sem.at[5])
     depth_copy.start()
     wait(finr.at[0], swap_r.at[7])
-    wait(finr.at[1:3], swap_r.at[8])
+    wait(finr.at[1], swap_r.at[8])
+    wait(finr.at[2], swap_r.at[5])
     rows_copy = pltpu.make_async_copy(finr, rows_out, out_sem.at[6])
     rows_copy.start()
-    wait(allq.at[across, lower], gy_r.at[0])
-    wait(allq.at[across, upper], gy_r.at[1])
+    put(left, 2)
+    put(right, 3)
+    for slot in range(ZN):
+        for side in range(2):
+            wait(allq.at[across, 0, side], gy_r.at[side, slot])
     put(across, 4)
 
     @pl.when(off)
@@ -673,7 +696,8 @@
         wait(mixed, mb_s.at[0])
         wait(dsum_send, dx_s.at[0])
         wait(fin.at[0], swap_s.at[7])
-        wait(fin.at[1:3], swap_s.at[8])
+        wait(fin.at[1], swap_s.at[8])
+        wait(fin.at[2], swap_s.at[5])
 
     for i in range(1, TN):
         wait(g_in, og_s.at[i])
@@ -682,7 +706,8 @@
             for part in range(2):
                 if distance < 4 or part == direction:
                     wait(kv.at[part, chunk], ring_s.at[direction, distance - 1, part])
-                    wait(sbuf.at[direction, 0, part], bs_s.at[direction, distance - 1, part])
+                    for rows in range(2):
+                        wait(mg_send.at[rows], bs_s.at[direction, distance - 1, 2 * part + rows])
     for slot in range(8):
         wait(kv.at[:, chunk], sib_s.at[slot])
         wait(xsend.at[slot], bx_s.at[slot])
@@ -701,7 +726,7 @@
         wait(zs.at[side, 3, side], gz_s.at[side, 3])
         for slot in range(ZN):
             wait(zs.at[side, 0], gx_s.at[side, slot])
-        wait(allq.at[xi, lower], gy_s.at[side])
+            wait(zs.at[side, 0, 0], gy_s.at[side, slot])
     for i in range(1, 5):
         wait(allq.at[xi], out_sem.at[i])
     depth_copy.wait()
@@ -710,7 +735,7 @@
 
 def finish(
     rows_in, quarters, depth_in, dq_out, dk_out, dv_out, point_out, depth_out,
-    blocks, cells, load, store, small,
+    blocks, cells, rows, depth, load, store, small,
 ):
     loads = [
         pltpu.make_async_copy(quarters.at[i // 2, :, i % 2], blocks.at[i], load.at[i])
@@ -718,14 +743,10 @@
     ]
     for copy in loads:
         copy.start()
-    others = [
-        pltpu.make_async_copy(rows_in.at[0], dq_out.at[0], small.at[0]),
-        pltpu.make_async_copy(rows_in.at[1], dk_out.at[0], small.at[1]),
-        pltpu.make_async_copy(rows_in.at[2], dv_out.at[0], small.at[2]),
-        pltpu.make_async_copy(depth_in, depth_out, small.at[3]),
-    ]
-    for copy in others:
-        copy.start()
+    rows_load = pltpu.make_async_copy(rows_in, rows, small.at[0])
+    rows_load.start()
+    depth_load = pltpu.make_async_copy(depth_in, depth, small.at[1])
+    depth_load.start()
     stores = []
     for i in range(TN):
         loads[i].wait()
@@ -736,7 +757,17 @@
             )
         )
         stores[i].start()
-    for copy in stores + others:
+    rows_load.wait()
+    depth_load.wait()
+    stores += [
+        pltpu.make_async_copy(rows.at[0], dq_out.at[0], small.at[2]),
+        pltpu.make_async_copy(rows.at[1], dk_out.at[0], small.at[3]),
+        pltpu.make_async_copy(rows.at[2], dv_out.at[0], small.at[4]),
+        pltpu.make_async_copy(depth, depth_out, small.at[5]),
+    ]
+    for copy in stores[TN:]:
+        copy.start()
+    for copy in stores:
         copy.wait()
 
 
@@ -788,14 +819,14 @@
         dma((2, 4, 2)), dma((2, 4, 2)),
         dma((8,)), dma((8,)),
         dma((2, 2)), dma((2, 2)),
-        dma((2, 4, 2)), dma((2, 4, 2)),
+        dma((2, 4, 4)), dma((2, 4, 4)),
         dma((8,)), dma((8,)),
         dma((XN,)), dma((XN,)),
         dma((XN,)), dma((XN,)),
         dma((2, 4)), dma((2, 4)),
         dma((2, 4)), dma((2, 4)),
         dma((2, ZN)), dma((2, ZN)),
-        dma((2,)), dma((2,)),
+        dma((2, ZN)), dma((2, ZN)),
         dma((XN,)), dma((XN,)),
         dma((XN,)), dma((XN,)),
         dma((ZN,)), dma((ZN,)),
@@ -828,9 +859,11 @@
         scratch_shapes=[
             pltpu.VMEM((TN, ZN, PIECE, COLS), BF16),
             pltpu.VMEM((TN, COLS, COLS), F32),
-            dma((TN,)), dma((TN,)), dma((4,)),
+            pltpu.VMEM((3, ROWS, COLS), BF16),
+            pltpu.VMEM(depth_kernel.shape, F32),
+            dma((TN,)), dma((TN,)), dma((6,)),
         ],
-        compiler_params=pltpu.CompilerParams(vmem_limit_bytes=32 * 1024 * 1024),
+        compiler_params=pltpu.CompilerParams(vmem_limit_bytes=60 * 1024 * 1024),
         name="write_outputs",
     )(rows, quarters, depth)
 

time: 134 us -> 126 us (0.940); the launches traced: 133 us -> 126 us
  local copies, waits for them, and re-layouts: 3.52 us -> 0 us
  Pallas kernels: 128 us -> 125 us
    pallas_call x1, Pallas kernels: 125 us -> 122 us  [local(): pl.pallas_call(body, out_shape=(jax.ShapeDtypeStruct((3, ROWS, COLS), BF1...]
    unnamed x6 -> x0, local copies, waits for them, and re-layouts: 3.52 us -> none
where the time goes in v4:
time: 126 us
  Pallas kernels  125 us (99%)
    pallas_call x1, Pallas kernels, local(): pl.pallas_call(body, out_shape=(jax.ShapeDtypeStruct((3, ROWS, COLS), BF1...  122 us
    pallas_call x1, Pallas kernels, local(): pl.pallas_call(finish, out_shape=(part, part, part, jax.ShapeDtypeStruct(...  3.54 us

profile of v4, /device:TPU:1, one launch (start us, length us, event | category | flops | bytes accessed | tf_op | source)
XLA Modules:
  0.0 126.0 jit_solution(10013065489843488595)
XLA Ops:
  0.6 121.7 %layer_backward.1 = (bf16[3,256,384]{2,1,0:T(8,128)(2,1)}, bf16[4,8,2,48,384]{4,3,2,1,0:T(8,128)(2,1)}, f32[27,384]{1,0:T(8,128)}) custom-call(bf16[256,384]{1,0:T(8,128)(2,1)} %bitcast.4, bf16[256,384]{1,0:T(8,128)(2,1)} %bitcast.5, bf16[256,384]{1,0:T(8,128)(2,1)} %bitcast.6, bf16[256,384]{1,0:T(8,128)(2,1)} %bitcast.7, bf16[384,3072]{1,0:T(8,128)(2,1)} %w_in.1, ...), custom_call_target="tpu_custom_call" | custom-call | tf_op jit(solution)/shard_map/layer_backward/pallas_call | solution.py:834
  122.3 3.5 %write_outputs.1 = (bf16[1,256,384]{2,1,0:T(8,128)(2,1)}, bf16[1,256,384]{2,1,0:T(8,128)(2,1)}, bf16[1,256,384]{2,1,0:T(8,128)(2,1)}, f32[384,3072]{1,0:T(8,128)}, f32[27,384]{1,0:T(8,128)}) custom-call(bf16[3,256,384]{2,1,0:T(8,128)(2,1)} %get-tuple-element.8.rows_in, bf16[4,8,2,48,384]{4,3,2,1,0:T(8,128)(2,1)} %get-tuple-element.9.quarters, ...), custom_call_target="tpu_custom_call" | custom-call | tf_op jit(solution)/shard_map/write_outputs/pallas_call | solution.py:850

commit v5 on v4

--- a/solution.py
+++ b/solution.py
@@ -342,8 +342,6 @@
         at_ext[2, :, lanes] = rows[FRAME:]
     halo(1, at_ext)
 
-    for frame in (1, 2):
-        spread_columns(shifted, at_ext, frame)
     for head in range(HEADS):
         lanes = slice(head * HD, (head + 1) * HD)
         attended = jnp.concatenate([at_ext[1, :, lanes], at_ext[2, :, lanes]], axis=0)
@@ -449,7 +447,8 @@
                 added = shared(slot) + rbuf[side, distance].astype(F32)
                 sbuf[side, distance - 1] = added.astype(BF16)
                 goal = lax.rem(z + ZN + 1 - 2 * side, ZN)
-                terms_to(side, distance, 0, (2 * goal + half, tp, dp))
+                for part in range(2):
+                    terms_to(side, distance, part, (2 * goal + half, tp, dp))
 
             for place, event in enumerate(events):
                 pl.when(i == place)(event)
@@ -464,7 +463,7 @@
 
     def mix():
         halo_wait(1, at_ext)
-        for frame in (0, 3):
+        for frame in range(4):
             spread_columns(shifted, at_ext, frame)
         for frame in range(2):
             for head in range(HEADS):
@@ -625,29 +624,31 @@
     def nothing():
         pass
 
-    bwd_pair(7, target, mix)
+    bwd_pair(7, target, nothing)
     total = shared(7).astype(BF16)
     sbuf[0, 3, 0] = total[0]
     sbuf[1, 3, 1] = total[1]
     for part in range(2):
         terms_to(0, 4, part, at_z(1))
         terms_to(1, 4, 2 + part, at_z(-1))
-    bwd_step(3, [tap_sums, nothing, nothing, both(*[terms_send(3, part) for part in (1, 2, 3)])])
+    mix()
+    bwd_step(3, [nothing, nothing, nothing, both(*[terms_send(3, part) for part in (2, 3)])])
+    tap_sums()
     products()
     z_first()
     bwd_step(2, [
         nothing,
         ev(z_next, 3),
         nothing,
-        both(ev(z_next, 2), terms_send(2, 1)),
+        both(ev(z_next, 2), terms_send(2, 2)),
     ])
     bwd_step(1, [
-        both(ev(z_next, 1), terms_send(2, 2)),
-        both(z_last, terms_send(2, 3)),
+        both(ev(z_next, 1), terms_send(2, 3)),
+        z_last,
         ev(z_gather, 1),
-        both(ev(z_gather, 2), terms_send(1, 1)),
+        both(ev(z_gather, 2), terms_send(1, 2)),
     ])
-    bwd_pair(0, chunk, both(ev(z_gather, 3), terms_send(1, 2), terms_send(1, 3), depth_z))
+    bwd_pair(0, chunk, both(terms_send(1, 3), ev(z_gather, 3), depth_z))
     for head in range(HEADS):
         lanes = slice(head * HD, (head + 1) * HD)
         fin[0, :, lanes] = (jnp.transpose(dq_acc[head]) * scaling).astype(BF16)
@@ -655,6 +656,8 @@
     z_gather_far()
     put(xi, 1)
     total = shared(0)
+    x_relay(3)
+    x_relay(6)
     for part in range(2):
         for side in range(2):
             terms_wait(side, 1, 2 * part)
@@ -663,9 +666,7 @@
         fin[1 + part] = done.astype(BF16)
         swap(8 if part == 0 else 5, fin.at[1 + part], finr.at[1 + part])
         if part == 0:
-            x_relay(3)
-            x_relay(6)
-    x_relay(7)
+            x_relay(7)
 
     sums = dz[0].astype(F32)
     for i in range(1, ZN):
@@ -741,13 +742,22 @@
         pltpu.make_async_copy(quarters.at[i // 2, :, i % 2], blocks.at[i], load.at[i])
         for i in range(TN)
     ]
-    for copy in loads:
-        copy.start()
     rows_load = pltpu.make_async_copy(rows_in, rows, small.at[0])
     rows_load.start()
     depth_load = pltpu.make_async_copy(depth_in, depth, small.at[1])
     depth_load.start()
-    stores = []
+    for copy in loads:
+        copy.start()
+    rows_load.wait()
+    depth_load.wait()
+    stores = [
+        pltpu.make_async_copy(rows.at[0], dq_out.at[0], small.at[2]),
+        pltpu.make_async_copy(rows.at[1], dk_out.at[0], small.at[3]),
+        pltpu.make_async_copy(rows.at[2], dv_out.at[0], small.at[4]),
+        pltpu.make_async_copy(depth, depth_out, small.at[5]),
+    ]
+    for copy in stores:
+        copy.start()
     for i in range(TN):
         loads[i].wait()
         cells[i] = blocks[i].reshape(COLS, COLS).astype(F32)
@@ -756,17 +766,7 @@
                 cells.at[i], point_out.at[:, i * COLS : (i + 1) * COLS], store.at[i]
             )
         )
-        stores[i].start()
-    rows_load.wait()
-    depth_load.wait()
-    stores += [
-        pltpu.make_async_copy(rows.at[0], dq_out.at[0], small.at[2]),
-        pltpu.make_async_copy(rows.at[1], dk_out.at[0], small.at[3]),
-        pltpu.make_async_copy(rows.at[2], dv_out.at[0], small.at[4]),
-        pltpu.make_async_copy(depth, depth_out, small.at[5]),
-    ]
-    for copy in stores[TN:]:
-        copy.start()
+        stores[-1].start()
     for copy in stores:
         copy.wait()
 

time: 126 us -> 126 us (level)
    pallas_call x1, Pallas kernels: 122 us -> 120 us  [local(): pl.pallas_call(body, out_shape=(jax.ShapeDtypeStruct((3, ROWS, COLS), BF1...]
where the time goes in v5:
time: 126 us; the launch traced here: 125 us
  Pallas kernels  125 us (99%)
    pallas_call x1, Pallas kernels, local(): pl.pallas_call(body, out_shape=(jax.ShapeDtypeStruct((3, ROWS, COLS), BF1...  120 us
    pallas_call x1, Pallas kernels, local(): pl.pallas_call(finish, out_shape=(part, part, part, jax.ShapeDtypeStruct(...  4.2 us

profile of v5, /device:TPU:1, one launch (start us, length us, event | category | flops | bytes accessed | tf_op | source)
XLA Modules:
  0.0 125.3 jit_solution(3830795864109982402)
XLA Ops:
  0.6 120.3 %layer_backward.1 = (bf16[3,256,384]{2,1,0:T(8,128)(2,1)}, bf16[4,8,2,48,384]{4,3,2,1,0:T(8,128)(2,1)}, f32[27,384]{1,0:T(8,128)}) custom-call(bf16[256,384]{1,0:T(8,128)(2,1)} %bitcast.4, bf16[256,384]{1,0:T(8,128)(2,1)} %bitcast.5, bf16[256,384]{1,0:T(8,128)(2,1)} %bitcast.6, bf16[256,384]{1,0:T(8,128)(2,1)} %bitcast.7, bf16[384,3072]{1,0:T(8,128)(2,1)} %w_in.1, ...), custom_call_target="tpu_custom_call" | custom-call | tf_op jit(solution)/shard_map/layer_backward/pallas_call | solution.py:834
  121.0 4.2 %write_outputs.1 = (bf16[1,256,384]{2,1,0:T(8,128)(2,1)}, bf16[1,256,384]{2,1,0:T(8,128)(2,1)}, bf16[1,256,384]{2,1,0:T(8,128)(2,1)}, f32[384,3072]{1,0:T(8,128)}, f32[27,384]{1,0:T(8,128)}) custom-call(bf16[3,256,384]{2,1,0:T(8,128)(2,1)} %get-tuple-element.8.rows_in, bf16[4,8,2,48,384]{4,3,2,1,0:T(8,128)(2,1)} %get-tuple-element.9.quarters, ...), custom_call_target="tpu_custom_call" | custom-call | tf_op jit(solution)/shard_map/write_outputs/pallas_call | solution.py:850

commit v6 on v4

--- a/solution.py
+++ b/solution.py
@@ -300,6 +300,11 @@
 
     fwd_step(3)
 
+    last = 2 * lax.rem(z + 4, ZN) + core
+    ring_wait(0, 4, 0, last)
+    ring_wait(1, 4, 1, last)
+    to_sibling(7, last)
+
     wait(kern, swap_r.at[3])
     halo_wait(0, mg_ext)
     for frame in range(4):
@@ -318,10 +323,6 @@
                 result = result + kern[tap : tap + 1, lanes] * window
             do[frame * FRAME : (frame + 1) * FRAME, lanes] = result.astype(BF16)
 
-    last = 2 * lax.rem(z + 4, ZN) + core
-    ring_wait(0, 4, 0, last)
-    ring_wait(1, 4, 1, last)
-    to_sibling(7, last)
 
     def far(i, carry):
         @pl.when(i == 1)

time: 126 us -> 126 us (level); the launches traced: 126 us -> 124 us
  Pallas kernels: 125 us -> 123 us
    pallas_call x1, Pallas kernels: 122 us -> 120 us  [local(): pl.pallas_call(body, out_shape=(jax.ShapeDtypeStruct((3, ROWS, COLS), BF1...]
where the time goes in v6:
time: 126 us; the launch traced here: 124 us
  Pallas kernels  123 us (98%)
    pallas_call x1, Pallas kernels, local(): pl.pallas_call(body, out_shape=(jax.ShapeDtypeStruct((3, ROWS, COLS), BF1...  120 us
    pallas_call x1, Pallas kernels, local(): pl.pallas_call(finish, out_shape=(part, part, part, jax.ShapeDtypeStruct(...  3.54 us

profile of v6, /device:TPU:1, one launch (start us, length us, event | category | flops | bytes accessed | tf_op | source)
XLA Modules:
  0.0 124.2 jit_solution(14537163497821985190)
XLA Ops:
  0.6 119.9 %layer_backward.1 = (bf16[3,256,384]{2,1,0:T(8,128)(2,1)}, bf16[4,8,2,48,384]{4,3,2,1,0:T(8,128)(2,1)}, f32[27,384]{1,0:T(8,128)}) custom-call(bf16[256,384]{1,0:T(8,128)(2,1)} %bitcast.4, bf16[256,384]{1,0:T(8,128)(2,1)} %bitcast.5, bf16[256,384]{1,0:T(8,128)(2,1)} %bitcast.6, bf16[256,384]{1,0:T(8,128)(2,1)} %bitcast.7, bf16[384,3072]{1,0:T(8,128)(2,1)} %w_in.1, ...), custom_call_target="tpu_custom_call" | custom-call | tf_op jit(solution)/shard_map/layer_backward/pallas_call | solution.py:835
  120.5 3.5 %write_outputs.1 = (bf16[1,256,384]{2,1,0:T(8,128)(2,1)}, bf16[1,256,384]{2,1,0:T(8,128)(2,1)}, bf16[1,256,384]{2,1,0:T(8,128)(2,1)}, f32[384,3072]{1,0:T(8,128)}, f32[27,384]{1,0:T(8,128)}) custom-call(bf16[3,256,384]{2,1,0:T(8,128)(2,1)} %get-tuple-element.8.rows_in, bf16[4,8,2,48,384]{4,3,2,1,0:T(8,128)(2,1)} %get-tuple-element.9.quarters, ...), custom_call_target="tpu_custom_call" | custom-call | tf_op jit(solution)/shard_map/write_outputs/pallas_call | solution.py:851
